TPU v7x, 32 devices: a whole 2x2x4 slice. The times are simulated.
32 devices in a mesh: sec: 2 (over x), seq: 4 (over z), mp: 4 (over y, core).
Axes of the slice: x: 2, y: 2, z: 4, core: 2. Of those that a mesh axis runs over, the one named last changes fastest.
Arguments:
- queries: bfloat16 [1024, 2048], P(('sec', 'seq'), 'mp'), may hold values from -6 to 6
- keys_values: bfloat16 [2, 16, 2048], P(None, ('sec', 'seq'), 'mp'), may hold values from -6 to 6
- out_grad: bfloat16 [1024, 4096], P(('sec', 'seq'), 'mp'), may hold values from -6 to 6
- out_weight: bfloat16 [2048, 4096], P('mp'), may hold values from -0.125 to 0.125
- enc_len: int32 [2], replicated, may hold values from 4 to 8
- dec_len: int32 [2], replicated, may hold values from 1 to 512
Outputs:
- query_grad: bfloat16 [1024, 2048], P(('sec', 'seq'), 'mp')
- key_value_grad: bfloat16 [2, 16, 2048], P(None, ('sec', 'seq'), 'mp')
All inputs are finite; a program needn't handle non-finite values.
Results may differ from a plain program's by a relative error of at most 0.014.
Values may be sent and summed in bfloat16 or wider, within the bound.
A program may use at most 64 MiB of HBM per device.

v0:
```python
import jax
import jax.numpy as jnp
from jax import lax
from jax.sharding import PartitionSpec as P

DH = 256
SEQS = 2


def body(queries, keys_values, out_grad, out_weight, enc_len, dec_len):
    score_scale = DH ** (-0.5)
    query_rows = queries.shape[0]
    local_width = queries.shape[1]
    heads_here = local_width // DH
    groups = lax.axis_size(("sec", "seq"))
    own_keys = keys_values.shape[1]
    total_k = own_keys * groups
    per_query_seq = query_rows * groups // SEQS
    per_key_seq = total_k // SEQS
    seq_ids = jnp.arange(SEQS, dtype=jnp.int32)
    query_pos = lax.axis_index(("sec", "seq")) * query_rows + jnp.arange(
        query_rows, dtype=jnp.int32
    )
    query_seg = query_pos // per_query_seq
    dec_limit = jnp.sum(
        jnp.where(query_seg[:, None] == seq_ids[None, :], dec_len[None, :], 0), axis=1
    )
    query_valid = query_pos % per_query_seq < dec_limit
    full_grad = lax.all_gather(out_grad, "mp", axis=1, tiled=True)
    grad_flat = jnp.dot(full_grad, out_weight.T, preferred_element_type=jnp.float32).astype(
        jnp.bfloat16
    )
    grad_flat = jnp.where(query_valid[:, None], grad_flat, jnp.zeros_like(grad_flat))
    q_heads = queries.reshape(query_rows, heads_here, DH)
    g_heads = grad_flat.reshape(query_rows, heads_here, DH)
    key_base = lax.axis_index("sec") * own_keys * lax.axis_size("seq")

    def allowed_for(key_width):
        key_pos = key_base + jnp.arange(key_width, dtype=jnp.int32)
        key_seg = key_pos // per_key_seq
        enc_limit = jnp.sum(
            jnp.where(key_seg[:, None] == seq_ids[None, :], enc_len[None, :], 0), axis=1
        )
        key_valid = key_pos % per_key_seq < enc_limit
        return (query_seg[:, None] == key_seg[None, :]) & key_valid[None, :]

    def scores_for(kv_block):
        key_width = kv_block.shape[1]
        k_heads = kv_block[0].reshape(key_width, heads_here, DH)
        v_heads = kv_block[1].reshape(key_width, heads_here, DH)
        scores = (
            jnp.einsum("qhd,khd->hqk", q_heads, k_heads, preferred_element_type=jnp.float32)
            * score_scale
        )
        allowed = allowed_for(key_width)[None]
        return (jnp.where(allowed, scores, -1e30), allowed, k_heads, v_heads)

    run_max = jnp.full((heads_here, query_rows), -1e30, jnp.float32)
    scores, allowed, k_heads, v_heads = scores_for(
        lax.all_gather(keys_values, "seq", axis=1, tiled=True)
    )
    new_max = jnp.maximum(run_max, jnp.max(scores, axis=2))
    expo_terms = jnp.where(allowed, jnp.exp(scores - new_max[..., None]), 0.0)
    run_total = jnp.sum(expo_terms, axis=2)
    weighted = jnp.einsum(
        "hqk,khd->hqd", expo_terms, v_heads.astype(jnp.float32), precision=lax.Precision.HIGHEST
    )
    run_max, run_total, weighted = (new_max, run_total, weighted)
    log_total = run_max + jnp.log(run_total)
    attn_out = weighted / run_total[..., None]
    row_delta = jnp.sum(jnp.transpose(g_heads.astype(jnp.float32), (1, 0, 2)) * attn_out, axis=2)
    kv_block = lax.all_gather(keys_values, "seq", axis=1, tiled=True)
    key_width = kv_block.shape[1]
    scores, allowed, k_heads, v_heads = scores_for(kv_block)
    attn_prob = jnp.where(allowed, jnp.exp(scores - log_total[..., None]), 0.0)
    grad_prob = jnp.einsum("qhd,khd->hqk", g_heads, v_heads, preferred_element_type=jnp.float32)
    grad_score = (attn_prob * (grad_prob - row_delta[..., None])).astype(jnp.bfloat16)
    grad_q = jnp.einsum("hqk,khd->hqd", grad_score, k_heads, preferred_element_type=jnp.float32)
    grad_key = (
        jnp.einsum("hqk,qhd->khd", grad_score, q_heads, preferred_element_type=jnp.float32)
        * score_scale
    )
    grad_value = jnp.einsum(
        "hqk,qhd->khd", attn_prob.astype(jnp.bfloat16), g_heads, preferred_element_type=jnp.float32
    )
    key_panel = jnp.stack(
        [grad_key.reshape(key_width, local_width), grad_value.reshape(key_width, local_width)]
    )
    grad_kv = key_panel
    grad_q, grad_kv = (grad_q, grad_kv)
    query_grad = (
        jnp.transpose(grad_q * score_scale, (1, 0, 2))
        .reshape(query_rows, local_width)
        .astype(jnp.bfloat16)
    )
    owned = lax.psum_scatter(grad_kv, "seq", scatter_dimension=1, tiled=True)
    return (query_grad, owned.astype(jnp.bfloat16))


def solution(mesh):
    placed = (
        P(("sec", "seq"), "mp"),
        P(None, ("sec", "seq"), "mp"),
        P(("sec", "seq"), "mp"),
        P("mp", None),
        P(),
        P(),
    )
    return jax.shard_map(
        body,
        mesh=mesh,
        in_specs=placed,
        out_specs=(P(("sec", "seq"), "mp"), P(None, ("sec", "seq"), "mp")),
        check_vma=False,
    )
```

profile of v0, /device:TPU:0, one launch (start us, length us, event | category | flops | bytes accessed | tf_op | source)
XLA Modules:
  0.0 61.5 jit_solution(13573505347506676959)
XLA Ops:
  7.2 0.0 copy-start
  7.2 0.0 all-gather.2.cloned.1.call-start
  7.2 0.7 %all-gather.2.cloned.1.call-update = ((bf16[128,1024]{1,0:T(8,128)(2,1)}), bf16[128,4096]{1,0:T(8,128)(2,1)}) async-update(((), (), s32[]{:S(2)}) %all-gather.2.cloned.1.call-start, bf16[128,1024]{1,0:T(8,128)(2,1)} %param.8) | async-update | bytes 1572888
  8.0 0.7 %copy.40 = bf16[2,2,512]{2,0,1:T(2,128)(2,1)S(1)} copy(bf16[2,2,512]{2,1,0:T(2,128)(2,1)} %param.7) | data formatting | bytes 8192 | tf_op args[1]
  8.7 14.8 %all_gather.7 = bf16[2,8,512]{2,0,1:T(2,128)(2,1)S(1)} all-gather(bf16[2,2,512]{2,0,1:T(2,128)(2,1)S(1)} %copy.40), channel_id=1, replica_groups=mesh['sec'=2,'seq'=4,'mp'=4] {'seq'}, dimensions={1}, use_global_device_ids=true | all-gather | bytes 20480 | tf_op jit(solution)/shard_map/all_gather | solution.py:72
  23.4 0.1 slice_reduce_fusion.1
  23.5 1.2 %dynamic-slice = u32[1]{0:T(128)} dynamic-slice(u32[32]{0:T(128)} %constant.92, u32[]{:T(128)S(6)} %add.89), dynamic_slice_sizes={1} | dynamic-slice | bytes 12
  25.4 0.7 %fusion.26 = s32[8]{0:T(128)S(1)} fusion(s32[2]{0:T(128)} %param.10, s32[8]{0:T(128)S(1)} %and_select_fusion.2), kind=kLoop, calls=%fused_computation.50 | loop fusion | flops 40 | bytes 72 | tf_op jit(solution)/shard_map/reduce_sum | solution.py:41
  26.2 0.1 compare_and_fusion
  26.3 1.0 %fusion.32 = (f32[2,128]{1,0:T(2,128)S(1)}, f32[2,128,8]{1,2,0:T(8,128)S(1)}) fusion(bf16[8,2,256]{2,0,1:T(8,128)(2,1)S(1)} %bitcast.46, bf16[16,2,8,256]{3,2,1,0:T(8,128)(2,1)} %bitcast.43, pred[128,8]{0,1:T(8,128)(4,1)S(1)} %compare_and_fusion), kind=kOutput, calls=%fused_computation.60 | convolution fusion | flops 1054464 | bytes 149504 | tf_op jit(solution)/shard_map/qhd,khd->hqk/dot_general | solution.py:52
  27.4 0.7 %fusion.27 = s32[128]{0:T(128)S(1)} fusion(s32[2]{0:T(128)} %param.11, s32[128]{0:T(128)S(1)} %and_select_fusion.3), kind=kLoop, calls=%fused_computation.51 | loop fusion | flops 640 | bytes 1032 | tf_op jit(solution)/shard_map/reduce_sum | solution.py:25
  28.1 0.9 %all-gather.2.cloned.1.call-done = bf16[128,4096]{1,0:T(8,128)(2,1)} async-done(((bf16[128,1024]{1,0:T(8,128)(2,1)}), bf16[128,4096]{1,0:T(8,128)(2,1)}) %all-gather.2.cloned.1.call-update) | async-done | bytes 1048592 | tf_op jit(solution)/shard_map/all_gather | solution.py:29
  29.0 4.0 %fusion.4 = bf16[128,512]{1,0:T(8,128)(2,1)S(1)} fusion(bf16[128,4096]{1,0:T(8,128)(2,1)} %all-gather.2.cloned.1.call-done, bf16[512,4096]{1,0:T(8,128)(2,1)} %param.9, pred[128]{0:T(512)(128)(4,1)S(1)} %fusion.29), kind=kOutput, calls=%fused_computation.7 | convolution fusion | flops 537001984 | bytes 5374080 | tf_op jit(solution)/shard_map/dot_general | solution.py:30
  33.1 0.4 fusion.2
  33.5 0.1 fusion.8
  33.6 0.1 fusion.7
  33.8 0.0 copy-done
  33.8 0.1 convolution_multiply_fusion.1
  33.9 0.2 fusion.3
  34.2 19.0 %all-reduce = bf16[2,8,512]{2,1,0:T(8,128)(2,1)S(1)} all-reduce(f32[2,8,512]{2,1,0:T(8,128)S(1)} %pad_maximum_fusion), channel_id=2, replica_groups=mesh['sec'=2,'seq'=4,'mp'=4] {'seq'}, use_global_device_ids=true, to_apply=%region_5.6.clone | all-reduce | flops 8192 | bytes 49152
  53.2 0.1 copy.48
  53.3 0.8 %copy.51 = bf16[128,512]{1,0:T(8,128)(2,1)} copy(bf16[128,512]{0,1:T(8,128)(2,1)S(1)} %bitcast.39) | data formatting | bytes 262144
  54.1 0.6 dynamic-slice_convert_fusion
  (8 shorter events, 0.1 us)
Async XLA Ops:
  7.2 26.6 %copy-start = (bf16[128,512]{1,0:T(8,128)(2,1)S(1)}, bf16[128,512]{1,0:T(8,128)(2,1)}, u32[]{:S(2)}) copy-start(bf16[128,512]{1,0:T(8,128)(2,1)} %param.6) | copy-start | bytes 393220
  7.2 21.9 %all-gather.2.cloned.1.call-start = ((), (), s32[]{:S(2)}) async-start(), calls=%async_computation | async-start | bytes 1310720 | tf_op jit(solution)/shard_map/all_gather | solution.py:29
Sparse Core Ops, SparseCore 0:
  9.6 19.4 all-gather.1
where the time goes:
time: 61.8 us; the launch traced here: 61.5 us
  blocking collectives  33.8 us (55%)
  between operations  14.8 us (24%)
  matrix products  6.15 us (10%)
  local copies, waits for them, and re-layouts  3.51 us (6%)
  other arithmetic  1.66 us (3%)
  waiting for transfers between devices  1.59 us (3%)
    unnamed x1, blocking collectives  19 us
    all_gather x1, blocking collectives, body(): kv_block = lax.all_gather(keys_values, 'seq', axis=1, tiled=True)  14.8 us
    dot_general x1, matrix products, body(): jnp.dot(full_grad, out_weight.T, preferred_element_type=jnp.float32)  4.04 us
    unnamed x5, local copies, waits for them, and re-layouts  2.72 us
  transfers between devices with their start and end apart: 1, of which 1 were waited for; matrix products, arithmetic and copies ran while one was open for 8% of the time, Pallas kernels for 0%

commit v1 on v0

v1 whole, which is shorter than its diff:
```python
import functools

import jax
import jax.numpy as jnp
from jax import lax
from jax.experimental import pallas as pl
from jax.experimental.pallas import tpu as pltpu
from jax.sharding import PartitionSpec as P

DH = 256
SEQS = 2
MESH = pl.DeviceIdType.MESH
NN = (((1,), (0,)), ((), ()))
NT = (((1,), (1,)), ((), ()))
TN = (((0,), (0,)), ((), ()))


def dot(a, b, dims):
    return lax.dot_general(a, b, dims, preferred_element_type=jnp.float32)


def kernel(
    seq_n,
    mp_n,
    enc_ref,
    dec_ref,
    q_hbm,
    kv_hbm,
    x_hbm,
    w_hbm,
    qg_hbm,
    kvg_ref,
    q_buf,
    x_buf,
    w_buf,
    kv_all,
    k_rows,
    v_rows,
    p_all,
    vw_send,
    vw_all,
    gp_send,
    gp_all,
    t_send,
    t_all,
    kvg_send,
    kvg_all,
    qg_buf,
    q_sem,
    x_sem,
    w_sem,
    kv_own_sem,
    qg_sem,
    kv_s,
    kv_r,
    p_s,
    p_r,
    vw_s,
    vw_r,
    gp_s,
    gp_r,
    t_s,
    t_r,
    kvg_s,
    kvg_r,
):
    sec = lax.axis_index("sec")
    seq = lax.axis_index("seq")
    mp = lax.axis_index("mp")
    rows, width = q_buf.shape
    cols = x_buf.shape[1]
    own = kv_hbm.shape[1]
    heads = width // DH
    keys = own * seq_n
    kh = heads * keys

    chips = mp_n // 2
    chip, core = mp // 2, mp % 2
    partners = []
    for step in list(range(1, chips)) + [0]:
        for flip in (0, 1):
            if step or flip:
                there = (core + flip) % 2
                partners.append(
                    (
                        ((chip + step) % chips) * 2 + there,
                        ((chip + chips - step) % chips) * 2 + there,
                    )
                )
    ring = [((seq + d) % seq_n, (seq + seq_n - d) % seq_n) for d in range(1, seq_n)]

    def to_mp(src, dst, send, recv, peer):
        return pltpu.make_async_remote_copy(
            src_ref=src,
            dst_ref=dst,
            send_sem=send,
            recv_sem=recv,
            device_id=(sec, seq, peer),
            device_id_type=MESH,
        )

    def to_seq(src, dst, send, recv, peer):
        return pltpu.make_async_remote_copy(
            src_ref=src,
            dst_ref=dst,
            send_sem=send,
            recv_sem=recv,
            device_id=(sec, peer, mp),
            device_id_type=MESH,
        )

    kv_load = pltpu.make_async_copy(kv_hbm, kv_all.at[seq], kv_own_sem)
    kv_load.start()
    q_load = pltpu.make_async_copy(q_hbm, q_buf, q_sem)
    q_load.start()
    w_loads = []
    for n, piece in enumerate([to for to, _ in partners] + [mp]):
        start = pl.multiple_of(piece * cols, cols)
        load = pltpu.make_async_copy(
            w_hbm.at[:, pl.ds(start, cols)], w_buf.at[piece], w_sem.at[n]
        )
        load.start()
        w_loads.append(load)
    x_load = pltpu.make_async_copy(x_hbm, x_buf, x_sem)
    x_load.start()

    barrier = pltpu.get_barrier_semaphore()
    for to, _ in partners:
        pl.semaphore_signal(barrier, inc=1, device_id=(sec, seq, to), device_id_type=MESH)
    for to, _ in ring:
        pl.semaphore_signal(barrier, inc=1, device_id=(sec, to, mp), device_id_type=MESH)
    pl.semaphore_wait(barrier, len(partners) + len(ring))

    kv_copies = []
    for d, (to, _) in enumerate(ring):
        copy = to_seq(kv_hbm, kv_all.at[seq], kv_s.at[d], kv_r.at[d], to)
        copy.start()
        kv_copies.append(copy)
    kv_load.wait()
    for copy in kv_copies:
        copy.wait_recv()
    for t in range(seq_n):
        for h in range(heads):
            at = pl.ds(h * keys + t * own, own)
            k_rows[at, :] = kv_all[t, 0].astype(jnp.float32)
            v_rows[at, :] = kv_all[t, 1].astype(jnp.float32)
    row_head = lax.broadcasted_iota(jnp.int32, (kh, width), 0) // keys
    col_head = lax.broadcasted_iota(jnp.int32, (kh, width), 1) // DH
    diagonal = row_head == col_head
    k_diag = jnp.where(diagonal, k_rows[...], 0.0).astype(jnp.bfloat16)
    v_diag = jnp.where(diagonal, v_rows[...], 0.0).astype(jnp.bfloat16)

    scale = DH ** (-0.5)
    q_load.wait()
    scores = dot(k_diag, q_buf[...], NT) * scale
    key_at = lax.broadcasted_iota(jnp.int32, (keys, rows), 0)
    token_at = lax.broadcasted_iota(jnp.int32, (1, rows), 1) + seq * rows
    allowed = key_at < enc_ref[sec]
    valid = token_at < dec_ref[sec]
    probs = []
    for h in range(heads):
        s = jnp.where(allowed, scores[h * keys : (h + 1) * keys], -1e30)
        e = jnp.where(allowed, jnp.exp(s - jnp.max(s, axis=0, keepdims=True)), 0.0)
        e = e / jnp.sum(e, axis=0, keepdims=True)
        probs.append(jnp.where(valid, e, 0.0))
    prob = jnp.concatenate(probs, axis=0) if heads > 1 else probs[0]
    p_all[mp] = prob.astype(jnp.bfloat16)
    p_copies = []
    for d, (to, _) in enumerate(partners):
        copy = to_mp(p_all.at[mp], p_all.at[mp], p_s.at[d], p_r.at[d], to)
        copy.start()
        p_copies.append(copy)

    vw_copies = []
    for d, (to, _) in enumerate(partners):
        w_loads[d].wait()
        vw_send[to] = dot(v_diag, w_buf[to], NN).astype(jnp.bfloat16)
        copy = to_mp(vw_send.at[to], vw_all.at[mp], vw_s.at[d], vw_r.at[d], to)
        copy.start()
        vw_copies.append(copy)
    w_loads[-1].wait()
    vw_all[mp] = dot(v_diag, w_buf[mp], NN).astype(jnp.bfloat16)

    x_load.wait()
    t_copies = []
    for d, (to, source) in enumerate(partners):
        p_copies[d].wait_recv()
        t_send[source] = dot(p_all[source], x_buf[...], NN).astype(jnp.bfloat16)
        copy = to_mp(t_send.at[source], t_all.at[mp], t_s.at[d], t_r.at[d], source)
        copy.start()
        t_copies.append(copy)
    t_all[mp] = dot(p_all[mp], x_buf[...], NN).astype(jnp.bfloat16)

    gp_copies = []
    for d, (to, source) in enumerate(partners):
        vw_copies[d].wait_recv()
        gp_send[source] = dot(vw_all[source], x_buf[...], NT)
        copy = to_mp(gp_send.at[source], gp_all.at[mp], gp_s.at[d], gp_r.at[d], source)
        copy.start()
        gp_copies.append(copy)
    grad_prob = dot(vw_all[mp], x_buf[...], NT)
    value_part = dot(t_all[mp], w_buf[mp], NT)
    for d, (to, _) in enumerate(partners):
        gp_copies[d].wait_recv()
        grad_prob += gp_all[to]

    grads = []
    for h in range(heads):
        at = slice(h * keys, (h + 1) * keys)
        delta = jnp.sum(prob[at] * grad_prob[at], axis=0, keepdims=True)
        grads.append(prob[at] * (grad_prob[at] - delta))
    grad_score = (jnp.concatenate(grads, axis=0) if heads > 1 else grads[0]).astype(jnp.bfloat16)
    key_part = dot(grad_score, q_buf[...], NN) * scale
    for d, (to, _) in enumerate(partners):
        t_copies[d].wait_recv()
        value_part += dot(t_all[to], w_buf[to], NT)

    def own_head(part):
        part = jnp.where(diagonal, part, 0.0)
        return sum(part[h * keys : (h + 1) * keys] for h in range(heads))

    key_part, value_part = own_head(key_part), own_head(value_part)
    for t in range(seq_n):
        kvg_send[t, pl.ds(0, own), :] = key_part[t * own : (t + 1) * own]
        kvg_send[t, pl.ds(own, own), :] = value_part[t * own : (t + 1) * own]
    kvg_copies = []
    for d, (to, _) in enumerate(ring):
        copy = to_seq(kvg_send.at[to], kvg_all.at[seq], kvg_s.at[d], kvg_r.at[d], to)
        copy.start()
        kvg_copies.append(copy)

    qg_buf[...] = (dot(grad_score, k_diag, TN) * scale).astype(jnp.bfloat16)
    qg_store = pltpu.make_async_copy(qg_buf, qg_hbm, qg_sem)
    qg_store.start()

    total = kvg_send[seq]
    for d, (_, source) in enumerate(ring):
        kvg_copies[d].wait_recv()
        total += kvg_all[source]
    kvg_ref[0] = total[:own].astype(jnp.bfloat16)
    kvg_ref[1] = total[own:].astype(jnp.bfloat16)

    for copy in kv_copies + p_copies + vw_copies + t_copies + gp_copies + kvg_copies:
        copy.wait_send()
    qg_store.wait()


def body(queries, keys_values, out_grad, out_weight, enc_len, dec_len):
    seq_n, mp_n = lax.axis_size("seq"), lax.axis_size("mp")
    rows, width = queries.shape
    cols = out_grad.shape[1]
    own = keys_values.shape[1]
    keys = own * seq_n
    kh = width // DH * keys
    bf16, f32 = jnp.bfloat16, jnp.float32
    any_space = pl.BlockSpec(memory_space=pl.ANY)
    smem = pl.BlockSpec(memory_space=pltpu.SMEM)
    dma = pltpu.SemaphoreType.DMA
    return pl.pallas_call(
        functools.partial(kernel, seq_n, mp_n),
        out_shape=(
            jax.ShapeDtypeStruct((rows, width), bf16),
            jax.ShapeDtypeStruct((2, own, width), bf16),
        ),
        in_specs=[smem, smem, any_space, any_space, any_space, any_space],
        out_specs=(any_space, pl.BlockSpec(memory_space=pltpu.VMEM)),
        scratch_shapes=[
            pltpu.VMEM((rows, width), bf16),
            pltpu.VMEM((rows, cols), bf16),
            pltpu.VMEM((mp_n, width, cols), bf16),
            pltpu.VMEM((seq_n, 2, own, width), bf16),
            pltpu.VMEM((kh, width), f32),
            pltpu.VMEM((kh, width), f32),
            pltpu.VMEM((mp_n, kh, rows), bf16),
            pltpu.VMEM((mp_n, kh, cols), bf16),
            pltpu.VMEM((mp_n, kh, cols), bf16),
            pltpu.VMEM((mp_n, kh, rows), f32),
            pltpu.VMEM((mp_n, kh, rows), f32),
            pltpu.VMEM((mp_n, kh, cols), bf16),
            pltpu.VMEM((mp_n, kh, cols), bf16),
            pltpu.VMEM((seq_n, 2 * own, width), f32),
            pltpu.VMEM((seq_n, 2 * own, width), f32),
            pltpu.VMEM((rows, width), bf16),
            dma,
            dma,
            dma((mp_n,)),
            dma,
            dma,
            dma((seq_n,)),
            dma((seq_n,)),
            dma((mp_n,)),
            dma((mp_n,)),
            dma((mp_n,)),
            dma((mp_n,)),
            dma((mp_n,)),
            dma((mp_n,)),
            dma((mp_n,)),
            dma((mp_n,)),
            dma((seq_n,)),
            dma((seq_n,)),
        ],
        compiler_params=pltpu.CompilerParams(
            collective_id=0, has_side_effects=True, vmem_limit_bytes=48 * 2**20
        ),
        name="cross_attention_backward",
    )(enc_len, dec_len, queries, keys_values, out_grad, out_weight)


def solution(mesh):
    assert mesh.shape["sec"] == SEQS
    placed = (
        P(("sec", "seq"), "mp"),
        P(None, ("sec", "seq"), "mp"),
        P(("sec", "seq"), "mp"),
        P("mp", None),
        P(),
        P(),
    )
    return jax.shard_map(
        body,
        mesh=mesh,
        in_specs=placed,
        out_specs=(P(("sec", "seq"), "mp"), P(None, ("sec", "seq"), "mp")),
        check_vma=False,
    )
```

time: 61.8 us -> 30.3 us (0.49)
  blocking collectives: 33.8 us -> 0 us
  Pallas kernels: 0 us -> 22.2 us
  between operations: 14.8 us -> 0.65 us
  matrix products: 6.15 us -> 0 us
  local copies, waits for them, and re-layouts: 3.51 us -> 7.28 us
  other arithmetic: 1.66 us -> 0 us
  waiting for transfers between devices: 1.59 us -> 0 us
    pallas_call x0 -> x1, Pallas kernels: none -> 22.2 us  [body(): pl.pallas_call(functools.partial(kernel, seq_n, mp_n), out_shape=(jax.Sha...]
    unnamed x1 -> x0, blocking collectives: 19 us -> none
    all_gather x1 -> x0, blocking collectives: 14.8 us -> none  [body(): kv_block = lax.all_gather(keys_values, 'seq', axis=1, tiled=True)]
    dot_general x7 -> x0, matrix products: 6.15 us -> none  [the longest x1 4.04 us: body(): jnp.dot(full_grad, out_weight.T, preferred_element_type=jnp.float32)]
    unnamed x5 -> x14, local copies, waits for them, and re-layouts: 2.72 us -> 7.28 us
    reduce_sum x3 -> x0, other arithmetic: 1.51 us -> none  [the longest x1 0.74 us: body(): jnp.sum(jnp.where(query_seg[:, None] == seq_ids[None, :], dec_len[None, :...]
    all_gather x1 -> x0, waiting for transfers between devices: 0.91 us -> none  [body(): full_grad = lax.all_gather(out_grad, 'mp', axis=1, tiled=True)]
    convert_element_type x2 -> x0, local copies, waits for them, and re-layouts: 0.72 us -> none  [the longest x1 0.6 us: body(): return (query_grad, owned.astype(jnp.bfloat16))]
  transfers between devices with their start and end apart: 1 -> 0, of which waited for: 1 -> 0; matrix products, arithmetic and copies ran while one was open for 8% -> 0% of each run, Pallas kernels for 0% -> 0%
where the time goes in v1:
time: 30.3 us; the launch traced here: 30.1 us
  Pallas kernels  22.2 us (73%)
  local copies, waits for them, and re-layouts  7.28 us (24%)
  between operations  0.65 us (2%)
    pallas_call x1, Pallas kernels, body(): pl.pallas_call(functools.partial(kernel, seq_n, mp_n), out_shape=(jax.Sha...  22.2 us
    unnamed x14, local copies, waits for them, and re-layouts  7.28 us

profile of v1, /device:TPU:0, one launch (start us, length us, event | category | flops | bytes accessed | tf_op | source)
XLA Modules:
  0.0 30.1 jit_solution(3961241252840990039)
XLA Ops:
  0.6 0.0 copy-start
  0.6 2.2 %copy-done = bf16[512,4096]{1,0:T(8,128)(2,1)S(1)} copy-done((bf16[512,4096]{1,0:T(8,128)(2,1)S(1)}, bf16[512,4096]{1,0:T(8,128)(2,1)}, u32[]{:S(2)}) %copy-start) | copy-done | bytes 4194328
  2.8 0.0 copy-start.1
  2.8 0.9 %copy-done.1 = bf16[128,1024]{1,0:T(8,128)(2,1)S(1)} copy-done((bf16[128,1024]{1,0:T(8,128)(2,1)S(1)}, bf16[128,1024]{1,0:T(8,128)(2,1)}, u32[]{:S(2)}) %copy-start.1) | copy-done | bytes 262168
  3.8 0.0 copy-start.2
  3.8 0.9 %copy-done.2 = bf16[128,512]{1,0:T(8,128)(2,1)S(1)} copy-done((bf16[128,512]{1,0:T(8,128)(2,1)S(1)}, bf16[128,512]{1,0:T(8,128)(2,1)}, u32[]{:S(2)}) %copy-start.2) | copy-done | bytes 131096
  4.7 0.0 copy-start.3
  4.7 0.7 %copy-done.3 = bf16[2,2,512]{2,1,0:T(2,128)(2,1)S(1)} copy-done((bf16[2,2,512]{2,1,0:T(2,128)(2,1)S(1)}, bf16[2,2,512]{2,1,0:T(2,128)(2,1)}, u32[]{:S(2)}) %copy-start.3) | copy-done | bytes 4120
  5.4 0.0 copy-start.4
  5.4 0.7 %copy-done.4 = s32[2]{0:T(128)S(1)} copy-done((s32[2]{0:T(128)S(1)}, s32[2]{0:T(128)}, u32[]{:S(2)}) %copy-start.4) | copy-done | bytes 32
  6.0 0.0 copy-start.5
  6.0 0.7 %copy-done.5 = s32[2]{0:T(128)S(1)} copy-done((s32[2]{0:T(128)S(1)}, s32[2]{0:T(128)}, u32[]{:S(2)}) %copy-start.5) | copy-done | bytes 32
  6.7 22.2 %cross_attention_backward.1 = (bf16[128,512]{1,0:T(8,128)(2,1)S(1)}, bf16[2,2,512]{2,1,0:T(2,128)(2,1)S(1)}) custom-call(s32[2]{0:T(128)S(1)} %copy-done.4, s32[2]{0:T(128)S(1)} %copy-done.5, bf16[128,512]{1,0:T(8,128)(2,1)S(1)} %copy-done.2, bf16[2,2,512]{2,1,0:T(2,128)(2,1)S(1)} %copy-done.3, bf16[128,1024]{1,0:T(8,128)(2,1)S(1)} %copy-done.1, ...), custom_call_target="tpu_custom_call" | custom-call | tf_op jit(solution)/shard_map/cross_attention_backward/pallas_call | solution.py:259
  28.8 0.7 %copy.10 = bf16[128,512]{1,0:T(8,128)(2,1)} copy(bf16[128,512]{1,0:T(8,128)(2,1)S(1)} %get-tuple-element.4) | data formatting | bytes 262144
  29.5 0.6 %copy.11 = bf16[2,2,512]{2,1,0:T(2,128)(2,1)} copy(bf16[2,2,512]{2,1,0:T(2,128)(2,1)S(1)} %get-tuple-element.5) | data formatting | bytes 8192
Async XLA Ops:
  0.6 2.2 %copy-start = (bf16[512,4096]{1,0:T(8,128)(2,1)S(1)}, bf16[512,4096]{1,0:T(8,128)(2,1)}, u32[]{:S(2)}) copy-start(bf16[512,4096]{1,0:T(8,128)(2,1)} %w_hbm.1) | copy-start | bytes 12582916
  2.8 0.9 %copy-start.1 = (bf16[128,1024]{1,0:T(8,128)(2,1)S(1)}, bf16[128,1024]{1,0:T(8,128)(2,1)}, u32[]{:S(2)}) copy-start(bf16[128,1024]{1,0:T(8,128)(2,1)} %x_hbm.1) | copy-start | bytes 786436
  3.8 0.9 %copy-start.2 = (bf16[128,512]{1,0:T(8,128)(2,1)S(1)}, bf16[128,512]{1,0:T(8,128)(2,1)}, u32[]{:S(2)}) copy-start(bf16[128,512]{1,0:T(8,128)(2,1)} %q_hbm.1) | copy-start | bytes 393220
  4.7 0.7 %copy-start.3 = (bf16[2,2,512]{2,1,0:T(2,128)(2,1)S(1)}, bf16[2,2,512]{2,1,0:T(2,128)(2,1)}, u32[]{:S(2)}) copy-start(bf16[2,2,512]{2,1,0:T(2,128)(2,1)} %kv_hbm.1) | copy-start | bytes 12292
  5.4 0.7 %copy-start.4 = (s32[2]{0:T(128)S(1)}, s32[2]{0:T(128)}, u32[]{:S(2)}) copy-start(s32[2]{0:T(128)} %enc_ref.1) | copy-start | bytes 28
  6.0 0.7 %copy-start.5 = (s32[2]{0:T(128)S(1)}, s32[2]{0:T(128)}, u32[]{:S(2)}) copy-start(s32[2]{0:T(128)} %dec_ref.1) | copy-start | bytes 28

commit v2 on v1

--- a/solution.py
+++ b/solution.py
@@ -22,14 +22,16 @@
 def kernel(
     seq_n,
     mp_n,
-    enc_ref,
-    dec_ref,
+    enc_hbm,
+    dec_hbm,
     q_hbm,
     kv_hbm,
     x_hbm,
     w_hbm,
     qg_hbm,
     kvg_ref,
+    enc_buf,
+    dec_buf,
     q_buf,
     x_buf,
     w_buf,
@@ -46,11 +48,12 @@
     kvg_send,
     kvg_all,
     qg_buf,
+    len_sem,
+    qg_sem,
     q_sem,
     x_sem,
     w_sem,
     kv_own_sem,
-    qg_sem,
     kv_s,
     kv_r,
     p_s,
@@ -109,6 +112,12 @@
             device_id_type=MESH,
         )
 
+    barrier = pltpu.get_barrier_semaphore()
+    for to, _ in partners:
+        pl.semaphore_signal(barrier, inc=1, device_id=(sec, seq, to), device_id_type=MESH)
+    for to, _ in ring:
+        pl.semaphore_signal(barrier, inc=1, device_id=(sec, to, mp), device_id_type=MESH)
+
     kv_load = pltpu.make_async_copy(kv_hbm, kv_all.at[seq], kv_own_sem)
     kv_load.start()
     q_load = pltpu.make_async_copy(q_hbm, q_buf, q_sem)
@@ -123,12 +132,11 @@
         w_loads.append(load)
     x_load = pltpu.make_async_copy(x_hbm, x_buf, x_sem)
     x_load.start()
-
-    barrier = pltpu.get_barrier_semaphore()
-    for to, _ in partners:
-        pl.semaphore_signal(barrier, inc=1, device_id=(sec, seq, to), device_id_type=MESH)
-    for to, _ in ring:
-        pl.semaphore_signal(barrier, inc=1, device_id=(sec, to, mp), device_id_type=MESH)
+    enc_load = pltpu.make_async_copy(enc_hbm, enc_buf, len_sem.at[0])
+    enc_load.start()
+    dec_load = pltpu.make_async_copy(dec_hbm, dec_buf, len_sem.at[1])
+    dec_load.start()
+
     pl.semaphore_wait(barrier, len(partners) + len(ring))
 
     kv_copies = []
@@ -155,8 +163,10 @@
     scores = dot(k_diag, q_buf[...], NT) * scale
     key_at = lax.broadcasted_iota(jnp.int32, (keys, rows), 0)
     token_at = lax.broadcasted_iota(jnp.int32, (1, rows), 1) + seq * rows
-    allowed = key_at < enc_ref[sec]
-    valid = token_at < dec_ref[sec]
+    enc_load.wait()
+    dec_load.wait()
+    allowed = key_at < enc_buf[sec]
+    valid = token_at < dec_buf[sec]
     probs = []
     for h in range(heads):
         s = jnp.where(allowed, scores[h * keys : (h + 1) * keys], -1e30)
@@ -182,24 +192,27 @@
     vw_all[mp] = dot(v_diag, w_buf[mp], NN).astype(jnp.bfloat16)
 
     x_load.wait()
+    for copy in p_copies:
+        copy.wait_recv()
+    t_rows = dot(p_all[...].reshape(mp_n * kh, rows), x_buf[...], NN)
+    t_send[...] = t_rows.astype(jnp.bfloat16).reshape(mp_n, kh, cols)
     t_copies = []
-    for d, (to, source) in enumerate(partners):
-        p_copies[d].wait_recv()
-        t_send[source] = dot(p_all[source], x_buf[...], NN).astype(jnp.bfloat16)
+    for d, (_, source) in enumerate(partners):
         copy = to_mp(t_send.at[source], t_all.at[mp], t_s.at[d], t_r.at[d], source)
         copy.start()
         t_copies.append(copy)
-    t_all[mp] = dot(p_all[mp], x_buf[...], NN).astype(jnp.bfloat16)
-
+
+    for copy in vw_copies:
+        copy.wait_recv()
+    gp_rows = dot(vw_all[...].reshape(mp_n * kh, cols), x_buf[...], NT)
+    gp_send[...] = gp_rows.reshape(mp_n, kh, rows)
     gp_copies = []
-    for d, (to, source) in enumerate(partners):
-        vw_copies[d].wait_recv()
-        gp_send[source] = dot(vw_all[source], x_buf[...], NT)
+    for d, (_, source) in enumerate(partners):
         copy = to_mp(gp_send.at[source], gp_all.at[mp], gp_s.at[d], gp_r.at[d], source)
         copy.start()
         gp_copies.append(copy)
-    grad_prob = dot(vw_all[mp], x_buf[...], NT)
-    value_part = dot(t_all[mp], w_buf[mp], NT)
+    grad_prob = gp_send[mp]
+    value_part = dot(t_send[mp], w_buf[mp], NT)
     for d, (to, _) in enumerate(partners):
         gp_copies[d].wait_recv()
         grad_prob += gp_all[to]
@@ -253,8 +266,8 @@
     keys = own * seq_n
     kh = width // DH * keys
     bf16, f32 = jnp.bfloat16, jnp.float32
-    any_space = pl.BlockSpec(memory_space=pl.ANY)
-    smem = pl.BlockSpec(memory_space=pltpu.SMEM)
+    hbm = pl.BlockSpec(memory_space=pltpu.HBM)
+    vmem = pl.BlockSpec(memory_space=pltpu.VMEM)
     dma = pltpu.SemaphoreType.DMA
     return pl.pallas_call(
         functools.partial(kernel, seq_n, mp_n),
@@ -262,9 +275,11 @@
             jax.ShapeDtypeStruct((rows, width), bf16),
             jax.ShapeDtypeStruct((2, own, width), bf16),
         ),
-        in_specs=[smem, smem, any_space, any_space, any_space, any_space],
-        out_specs=(any_space, pl.BlockSpec(memory_space=pltpu.VMEM)),
+        in_specs=[hbm] * 6,
+        out_specs=(hbm, vmem),
         scratch_shapes=[
+            pltpu.SMEM((SEQS,), jnp.int32),
+            pltpu.SMEM((SEQS,), jnp.int32),
             pltpu.VMEM((rows, width), bf16),
             pltpu.VMEM((rows, cols), bf16),
             pltpu.VMEM((mp_n, width, cols), bf16),
@@ -281,10 +296,11 @@
             pltpu.VMEM((seq_n, 2 * own, width), f32),
             pltpu.VMEM((seq_n, 2 * own, width), f32),
             pltpu.VMEM((rows, width), bf16),
+            dma((2,)),
             dma,
             dma,
-            dma((mp_n,)),
             dma,
+            dma((mp_n,)),
             dma,
             dma((seq_n,)),
             dma((seq_n,)),
@@ -300,7 +316,7 @@
             dma((seq_n,)),
         ],
         compiler_params=pltpu.CompilerParams(
-            collective_id=0, has_side_effects=True, vmem_limit_bytes=48 * 2**20
+            collective_id=0, has_side_effects=True, vmem_limit_bytes=63 * 2**20
         ),
         name="cross_attention_backward",
     )(enc_len, dec_len, queries, keys_values, out_grad, out_weight)

time: 30.3 us -> 25.4 us (0.84)
  local copies, waits for them, and re-layouts: 7.28 us -> 2.85 us
  Pallas kernels: 22.2 us -> 21.7 us
    unnamed x14 -> x2, local copies, waits for them, and re-layouts: 7.28 us -> 2.85 us
    pallas_call x1, Pallas kernels: 22.2 us -> 21.7 us  [body(): pl.pallas_call(functools.partial(kernel, seq_n, mp_n), out_shape=(jax.Sha...]
where the time goes in v2:
time: 25.4 us; the launch traced here: 25.2 us
  Pallas kernels  21.7 us (85%)
  local copies, waits for them, and re-layouts  2.85 us (11%)
  between operations  0.64 us (3%)
    pallas_call x1, Pallas kernels, body(): pl.pallas_call(functools.partial(kernel, seq_n, mp_n), out_shape=(jax.Sha...  21.7 us
    unnamed x2, local copies, waits for them, and re-layouts  2.85 us

profile of v2, /device:TPU:0, one launch (start us, length us, event | category | flops | bytes accessed | tf_op | source)
XLA Modules:
  0.0 25.2 jit_solution(3612916276906538031)
XLA Ops:
  0.6 21.7 %cross_attention_backward.1 = (bf16[128,512]{1,0:T(8,128)(2,1)}, bf16[2,2,512]{2,1,0:T(2,128)(2,1)}) custom-call(s32[2]{0:T(128)} %enc_hbm.1, s32[2]{0:T(128)} %dec_hbm.1, bf16[128,512]{1,0:T(8,128)(2,1)} %q_hbm.1, bf16[2,2,512]{2,1,0:T(2,128)(2,1)} %kv_hbm.1, bf16[128,1024]{1,0:T(8,128)(2,1)} %x_hbm.1, bf16[512,4096]{1,0:T(8,128)(2,1)} %w_hbm.1), custom_call_target="tpu_custom_call" | custom-call | tf_op jit(solution)/shard_map/cross_attention_backward/pallas_call | solution.py:272
  22.3 1.6 %copy.10 = bf16[128,512]{1,0:T(8,128)(2,1)} copy(bf16[128,512]{1,0:T(8,128)(2,1)} %get-tuple-element.4) | data formatting | bytes 262144
  23.9 1.3 %copy.11 = bf16[2,2,512]{2,1,0:T(2,128)(2,1)} copy(bf16[2,2,512]{2,1,0:T(2,128)(2,1)} %get-tuple-element.5) | data formatting | bytes 8192

commit v3 on v1

v3 whole, which is shorter than its diff:
```python
import functools

import jax
import jax.numpy as jnp
from jax import lax
from jax.experimental import pallas as pl
from jax.experimental.pallas import tpu as pltpu
from jax.sharding import PartitionSpec as P

DH = 256
SEQS = 2
CHUNK = 256
MESH = pl.DeviceIdType.MESH
NN = (((1,), (0,)), ((), ()))
NT = (((1,), (1,)), ((), ()))
TN = (((0,), (0,)), ((), ()))


def dot(a, b, dims):
    return lax.dot_general(a, b, dims, preferred_element_type=jnp.float32)


def kernel(
    seq_n,
    mp_n,
    enc_hbm,
    dec_hbm,
    q_hbm,
    kv_hbm,
    x_hbm,
    w_hbm,
    qg_ref,
    kvg_ref,
    enc_buf,
    dec_buf,
    q_buf,
    x_all,
    w_buf,
    kv_all,
    k_rows,
    v_rows,
    g_sum,
    kvg_send,
    kvg_all,
    len_sem,
    q_sem,
    x_sem,
    w_sem,
    kv_own_sem,
    kv_s,
    kv_r,
    pair_s,
    pair_r,
    far_s,
    far_r,
    pass_s,
    pass_r,
    kvg_s,
    kvg_r,
):
    sec = lax.axis_index("sec")
    seq = lax.axis_index("seq")
    mp = lax.axis_index("mp")
    rows, width = q_buf.shape
    chunks = x_all.shape[1]
    cols = chunks * CHUNK
    own = kv_hbm.shape[1]
    heads = width // DH
    keys = own * seq_n
    kh = heads * keys

    chips = mp_n // 2
    chip, core = mp // 2, mp % 2
    pair = chip * 2 + 1 - core
    far = [
        (((chip + d) % chips) * 2 + core, ((chip + chips - d) % chips) * 2 + core)
        for d in range(1, chips)
    ]
    ring = [((seq + d) % seq_n, (seq + seq_n - d) % seq_n) for d in range(1, seq_n)]

    def to_mp(src, dst, send, recv, peer):
        return pltpu.make_async_remote_copy(
            src_ref=src,
            dst_ref=dst,
            send_sem=send,
            recv_sem=recv,
            device_id=(sec, seq, peer),
            device_id_type=MESH,
        )

    def to_seq(src, dst, send, recv, peer):
        return pltpu.make_async_remote_copy(
            src_ref=src,
            dst_ref=dst,
            send_sem=send,
            recv_sem=recv,
            device_id=(sec, peer, mp),
            device_id_type=MESH,
        )

    barrier = pltpu.get_barrier_semaphore()
    for to in [pair] + [to for to, _ in far]:
        pl.semaphore_signal(barrier, inc=1, device_id=(sec, seq, to), device_id_type=MESH)
    for to, _ in ring:
        pl.semaphore_signal(barrier, inc=1, device_id=(sec, to, mp), device_id_type=MESH)

    kv_load = pltpu.make_async_copy(kv_hbm, kv_all.at[seq], kv_own_sem)
    kv_load.start()
    q_load = pltpu.make_async_copy(q_hbm, q_buf, q_sem)
    q_load.start()
    enc_load = pltpu.make_async_copy(enc_hbm, enc_buf, len_sem.at[0])
    enc_load.start()
    dec_load = pltpu.make_async_copy(dec_hbm, dec_buf, len_sem.at[1])
    dec_load.start()
    x_loads = []
    for c in range(chunks):
        load = pltpu.make_async_copy(
            x_hbm.at[:, pl.ds(c * CHUNK, CHUNK)], x_all.at[mp, c], x_sem.at[c]
        )
        load.start()
        x_loads.append(load)
    order = [mp, pair] + [source for _, source in far]
    for _, source in far:
        order.append((source // 2) * 2 + 1 - core)
    w_loads = []
    for n, piece in enumerate(order):
        start = pl.multiple_of(piece * cols, cols)
        load = pltpu.make_async_copy(
            w_hbm.at[:, pl.ds(start, cols)], w_buf.at[piece], w_sem.at[n]
        )
        load.start()
        w_loads.append(load)

    pl.semaphore_wait(barrier, 1 + len(far) + len(ring))

    kv_copies = []
    for d, (to, _) in enumerate(ring):
        copy = to_seq(kv_hbm, kv_all.at[seq], kv_s.at[d], kv_r.at[d], to)
        copy.start()
        kv_copies.append(copy)
    far_copies = {}
    pair_copies = []
    for c in range(chunks):
        part = x_hbm.at[:, pl.ds(c * CHUNK, CHUNK)]
        for d, (to, _) in enumerate(far):
            copy = to_mp(part, x_all.at[mp, c], far_s.at[d, c], far_r.at[d, c], to)
            copy.start()
            far_copies[d, c] = copy
        copy = to_mp(part, x_all.at[mp, c], pair_s.at[c], pair_r.at[c], pair)
        copy.start()
        pair_copies.append(copy)

    def part_of(source, c):
        return dot(x_all[source, c], w_buf[source, :, c * CHUNK : (c + 1) * CHUNK], NT)

    for load in x_loads:
        load.wait()
    w_loads[0].wait()
    total = part_of(mp, 0)
    for c in range(1, chunks):
        total += part_of(mp, c)
    g_sum[...] = total

    for copy in pair_copies:
        copy.wait_recv()
    w_loads[1].wait()
    total = g_sum[...]
    for c in range(chunks):
        total += part_of(pair, c)
    g_sum[...] = total

    kv_load.wait()
    for copy in kv_copies:
        copy.wait_recv()
    for t in range(seq_n):
        for h in range(heads):
            at = pl.ds(h * keys + t * own, own)
            k_rows[at, :] = kv_all[t, 0].astype(jnp.float32)
            v_rows[at, :] = kv_all[t, 1].astype(jnp.float32)
    row_head = lax.broadcasted_iota(jnp.int32, (kh, width), 0) // keys
    col_head = lax.broadcasted_iota(jnp.int32, (kh, width), 1) // DH
    diagonal = row_head == col_head
    k_diag = jnp.where(diagonal, k_rows[...], 0.0).astype(jnp.bfloat16)
    v_diag = jnp.where(diagonal, v_rows[...], 0.0).astype(jnp.bfloat16)

    scale = DH ** (-0.5)
    q_load.wait()
    scores = dot(k_diag, q_buf[...], NT) * scale
    key_at = lax.broadcasted_iota(jnp.int32, (keys, rows), 0)
    token_at = lax.broadcasted_iota(jnp.int32, (1, rows), 1) + seq * rows
    enc_load.wait()
    dec_load.wait()
    allowed = key_at < enc_buf[sec]
    valid = token_at < dec_buf[sec]
    probs = []
    for h in range(heads):
        s = jnp.where(allowed, scores[h * keys : (h + 1) * keys], -1e30)
        e = jnp.where(allowed, jnp.exp(s - jnp.max(s, axis=0, keepdims=True)), 0.0)
        e = e / jnp.sum(e, axis=0, keepdims=True)
        probs.append(jnp.where(valid, e, 0.0))
    prob = jnp.concatenate(probs, axis=0) if heads > 1 else probs[0]
    prob_bf16 = prob.astype(jnp.bfloat16)

    for load in w_loads[2:]:
        load.wait()
    pass_copies = {}
    for c in range(chunks + 1):
        if c < chunks:
            for d, (_, source) in enumerate(far):
                far_copies[d, c].wait_recv()
                slot = x_all.at[source, c]
                copy = to_mp(slot, slot, pass_s.at[d, c], pass_r.at[d, c], pair)
                copy.start()
                pass_copies[d, c] = copy
        total = g_sum[...]
        if c < chunks:
            for _, source in far:
                total += part_of(source, c)
        if c > 0:
            for d, (_, source) in enumerate(far):
                pass_copies[d, c - 1].wait_recv()
                total += part_of((source // 2) * 2 + 1 - core, c - 1)
        if c < chunks:
            g_sum[...] = total
    g = total.astype(jnp.bfloat16)

    value_part = dot(prob_bf16, g, NN)
    grad_prob = dot(v_diag, g, NT)
    grads = []
    for h in range(heads):
        at = slice(h * keys, (h + 1) * keys)
        delta = jnp.sum(prob[at] * grad_prob[at], axis=0, keepdims=True)
        grads.append(prob[at] * (grad_prob[at] - delta))
    grad_score = (jnp.concatenate(grads, axis=0) if heads > 1 else grads[0]).astype(jnp.bfloat16)
    key_part = dot(grad_score, q_buf[...], NN) * scale

    def own_head(part):
        part = jnp.where(diagonal, part, 0.0)
        return sum(part[h * keys : (h + 1) * keys] for h in range(heads))

    key_part, value_part = own_head(key_part), own_head(value_part)
    for t in range(seq_n):
        kvg_send[t, pl.ds(0, own), :] = key_part[t * own : (t + 1) * own]
        kvg_send[t, pl.ds(own, own), :] = value_part[t * own : (t + 1) * own]
    kvg_copies = []
    for d, (to, _) in enumerate(ring):
        copy = to_seq(kvg_send.at[to], kvg_all.at[seq], kvg_s.at[d], kvg_r.at[d], to)
        copy.start()
        kvg_copies.append(copy)

    qg_ref[...] = (dot(grad_score, k_diag, TN) * scale).astype(jnp.bfloat16)

    total = kvg_send[seq]
    for d, (_, source) in enumerate(ring):
        kvg_copies[d].wait_recv()
        total += kvg_all[source]
    kvg_ref[0] = total[:own].astype(jnp.bfloat16)
    kvg_ref[1] = total[own:].astype(jnp.bfloat16)

    sent = kv_copies + pair_copies + kvg_copies
    for copy in sent + list(far_copies.values()) + list(pass_copies.values()):
        copy.wait_send()


def store_kernel(qg_ref, kvg_ref, qg_hbm, kvg_hbm, sem):
    copies = [
        pltpu.make_async_copy(qg_ref, qg_hbm, sem.at[0]),
        pltpu.make_async_copy(kvg_ref, kvg_hbm, sem.at[1]),
    ]
    for copy in copies:
        copy.start()
    for copy in copies:
        copy.wait()


def body(queries, keys_values, out_grad, out_weight, enc_len, dec_len):
    seq_n, mp_n = lax.axis_size("seq"), lax.axis_size("mp")
    rows, width = queries.shape
    cols = out_grad.shape[1]
    chunks = cols // CHUNK
    own = keys_values.shape[1]
    keys = own * seq_n
    kh = width // DH * keys
    far_n = max(mp_n // 2 - 1, 1)
    bf16, f32 = jnp.bfloat16, jnp.float32
    hbm = pl.BlockSpec(memory_space=pltpu.HBM)
    vmem = pl.BlockSpec(memory_space=pltpu.VMEM)
    dma = pltpu.SemaphoreType.DMA
    operands = [
        pltpu.with_memory_space_constraint(a, pltpu.HBM)
        for a in (enc_len, dec_len, queries, keys_values, out_grad, out_weight)
    ]
    results = pl.pallas_call(
        functools.partial(kernel, seq_n, mp_n),
        out_shape=(
            pltpu.VMEM((rows, width), bf16),
            pltpu.VMEM((2, own, width), bf16),
        ),
        in_specs=[hbm] * 6,
        out_specs=(vmem, vmem),
        scratch_shapes=[
            pltpu.SMEM((SEQS,), jnp.int32),
            pltpu.SMEM((SEQS,), jnp.int32),
            pltpu.VMEM((rows, width), bf16),
            pltpu.VMEM((mp_n, chunks, rows, CHUNK), bf16),
            pltpu.VMEM((mp_n, width, cols), bf16),
            pltpu.VMEM((seq_n, 2, own, width), bf16),
            pltpu.VMEM((kh, width), f32),
            pltpu.VMEM((kh, width), f32),
            pltpu.VMEM((rows, width), f32),
            pltpu.VMEM((seq_n, 2 * own, width), f32),
            pltpu.VMEM((seq_n, 2 * own, width), f32),
            dma((2,)),
            dma,
            dma((chunks,)),
            dma((mp_n,)),
            dma,
            dma((seq_n,)),
            dma((seq_n,)),
            dma((chunks,)),
            dma((chunks,)),
            dma((far_n, chunks)),
            dma((far_n, chunks)),
            dma((far_n, chunks)),
            dma((far_n, chunks)),
            dma((seq_n,)),
            dma((seq_n,)),
        ],
        compiler_params=pltpu.CompilerParams(
            collective_id=0, has_side_effects=True, vmem_limit_bytes=48 * 2**20
        ),
        name="cross_attention_backward",
    )(*operands)
    return pl.pallas_call(
        store_kernel,
        out_shape=(
            jax.ShapeDtypeStruct((rows, width), bf16),
            jax.ShapeDtypeStruct((2, own, width), bf16),
        ),
        in_specs=[vmem, vmem],
        out_specs=(hbm, hbm),
        scratch_shapes=[dma((2,))],
        name="store_results",
    )(*results)


def solution(mesh):
    assert mesh.shape["sec"] == SEQS
    placed = (
        P(("sec", "seq"), "mp"),
        P(None, ("sec", "seq"), "mp"),
        P(("sec", "seq"), "mp"),
        P("mp", None),
        P(),
        P(),
    )
    return jax.shard_map(
        body,
        mesh=mesh,
        in_specs=placed,
        out_specs=(P(("sec", "seq"), "mp"), P(None, ("sec", "seq"), "mp")),
        check_vma=False,
    )
```

time: 30.3 us -> 20.5 us (0.68)
  local copies, waits for them, and re-layouts: 7.28 us -> 1.23 us
  Pallas kernels: 22.2 us -> 18.4 us
    unnamed x14 -> x4, local copies, waits for them, and re-layouts: 7.28 us -> 1.23 us
    pallas_call x1 -> x2, Pallas kernels: 22.2 us -> 18.4 us  [the longest x1 16.9 us: body(): pl.pallas_call(functools.partial(kernel, seq_n, mp_n), out_shape=(pltpu.V...]
where the time goes in v3:
time: 20.5 us; the launch traced here: 20.3 us
  Pallas kernels  18.4 us (90%)
  local copies, waits for them, and re-layouts  1.23 us (6%)
  between operations  0.65 us (3%)
    pallas_call x1, Pallas kernels, body(): pl.pallas_call(functools.partial(kernel, seq_n, mp_n), out_shape=(pltpu.V...  16.9 us
    pallas_call x1, Pallas kernels, body(): pl.pallas_call(store_kernel, out_shape=(jax.ShapeDtypeStruct((rows, width...  1.58 us
    unnamed x4, local copies, waits for them, and re-layouts  1.23 us

profile of v3, /device:TPU:0, one launch (start us, length us, event | category | flops | bytes accessed | tf_op | source)
XLA Modules:
  0.0 20.3 jit_solution(9250044334714842203)
XLA Ops:
  0.6 16.9 %cross_attention_backward.1 = (bf16[128,512]{1,0:T(8,128)(2,1)S(1)}, bf16[2,2,512]{2,1,0:T(2,128)(2,1)S(1)}) custom-call(s32[2]{0:T(128)} %enc_hbm.1, s32[2]{0:T(128)} %dec_hbm.1, bf16[128,512]{1,0:T(8,128)(2,1)} %q_hbm.1, bf16[2,2,512]{2,1,0:T(2,128)(2,1)} %kv_hbm.1, bf16[128,1024]{1,0:T(8,128)(2,1)} %x_hbm.1, bf16[512,4096]{1,0:T(8,128)(2,1)} %w_hbm.1), custom_call_target="tpu_custom_call" | custom-call | tf_op jit(solution)/shard_map/cross_attention_backward/pallas_call | solution.py:293
  17.5 0.0 copy-start
  17.5 0.6 %copy-done = bf16[128,512]{1,0:T(8,128)(2,1)} copy-done((bf16[128,512]{1,0:T(8,128)(2,1)}, bf16[128,512]{1,0:T(8,128)(2,1)S(1)}, u32[]{:S(2)}) %copy-start) | copy-done | bytes 131096
  18.2 0.0 copy-start.1
  18.2 0.6 %copy-done.1 = bf16[2,2,512]{2,1,0:T(2,128)(2,1)} copy-done((bf16[2,2,512]{2,1,0:T(2,128)(2,1)}, bf16[2,2,512]{2,1,0:T(2,128)(2,1)S(1)}, u32[]{:S(2)}) %copy-start.1) | copy-done | bytes 4120
  18.7 1.6 %store_results.1 = (bf16[128,512]{1,0:T(8,128)(2,1)}, bf16[2,2,512]{2,1,0:T(2,128)(2,1)}) custom-call(bf16[128,512]{1,0:T(8,128)(2,1)} %copy-done, bf16[2,2,512]{2,1,0:T(2,128)(2,1)} %copy-done.1), custom_call_target="tpu_custom_call" | custom-call | tf_op jit(solution)/shard_map/store_results/pallas_call | solution.py:334
Async XLA Ops:
  17.5 0.6 %copy-start = (bf16[128,512]{1,0:T(8,128)(2,1)}, bf16[128,512]{1,0:T(8,128)(2,1)S(1)}, u32[]{:S(2)}) copy-start(bf16[128,512]{1,0:T(8,128)(2,1)S(1)} %get-tuple-element.4.qg_ref) | copy-start | bytes 393220
  18.2 0.6 %copy-start.1 = (bf16[2,2,512]{2,1,0:T(2,128)(2,1)}, bf16[2,2,512]{2,1,0:T(2,128)(2,1)S(1)}, u32[]{:S(2)}) copy-start(bf16[2,2,512]{2,1,0:T(2,128)(2,1)S(1)} %get-tuple-element.5.kvg_ref) | copy-start | bytes 12292

commit v4 on v3

--- a/solution.py
+++ b/solution.py
@@ -9,7 +9,7 @@
 
 DH = 256
 SEQS = 2
-CHUNK = 256
+LANES = 128
 MESH = pl.DeviceIdType.MESH
 NN = (((1,), (0,)), ((), ()))
 NT = (((1,), (1,)), ((), ()))
@@ -18,6 +18,14 @@
 
 def dot(a, b, dims):
     return lax.dot_general(a, b, dims, preferred_element_type=jnp.float32)
+
+
+def pieces_of(cols):
+    edges = list(range(0, cols, max(cols // 4, LANES))) + [cols]
+    middle = (edges[-2] + cols) // 2
+    if middle % LANES == 0 and middle > edges[-2]:
+        edges.insert(-1, middle)
+    return list(zip(edges[:-1], edges[1:]))
 
 
 def kernel(
@@ -53,6 +61,8 @@
     pair_r,
     far_s,
     far_r,
+    cross_s,
+    cross_r,
     pass_s,
     pass_r,
     kvg_s,
@@ -62,8 +72,9 @@
     seq = lax.axis_index("seq")
     mp = lax.axis_index("mp")
     rows, width = q_buf.shape
-    chunks = x_all.shape[1]
-    cols = chunks * CHUNK
+    cols = x_all.shape[2]
+    pieces = pieces_of(cols)
+    last = len(pieces) - 1
     own = kv_hbm.shape[1]
     heads = width // DH
     keys = own * seq_n
@@ -76,6 +87,7 @@
         (((chip + d) % chips) * 2 + core, ((chip + chips - d) % chips) * 2 + core)
         for d in range(1, chips)
     ]
+    cross = [(to + 1 - 2 * core, source + 1 - 2 * core) for to, source in far]
     ring = [((seq + d) % seq_n, (seq + seq_n - d) % seq_n) for d in range(1, seq_n)]
 
     def to_mp(src, dst, send, recv, peer):
@@ -99,10 +111,35 @@
         )
 
     barrier = pltpu.get_barrier_semaphore()
-    for to in [pair] + [to for to, _ in far]:
+    for to in [pair] + [to for to, _ in far + cross]:
         pl.semaphore_signal(barrier, inc=1, device_id=(sec, seq, to), device_id_type=MESH)
     for to, _ in ring:
         pl.semaphore_signal(barrier, inc=1, device_id=(sec, to, mp), device_id_type=MESH)
+
+    pl.semaphore_wait(barrier, 1 + 2 * len(far) + len(ring))
+
+    kv_copies = []
+    for d, (to, _) in enumerate(ring):
+        copy = to_seq(kv_hbm, kv_all.at[seq], kv_s.at[d], kv_r.at[d], to)
+        copy.start()
+        kv_copies.append(copy)
+    far_copies = {}
+    for c, (start, end) in enumerate(pieces):
+        at = (slice(None), pl.ds(start, end - start))
+        for d, (to, _) in enumerate(far):
+            copy = to_mp(
+                x_hbm.at[at], x_all.at[(mp,) + at], far_s.at[d, c], far_r.at[d, c], to
+            )
+            copy.start()
+            far_copies[d, c] = copy
+        if c == 0:
+            pair_copy = to_mp(x_hbm, x_all.at[mp], pair_s, pair_r, pair)
+            pair_copy.start()
+    cross_copies = []
+    for d, (to, _) in enumerate(cross):
+        copy = to_mp(x_hbm.at[at], x_all.at[(mp,) + at], cross_s.at[d], cross_r.at[d], to)
+        copy.start()
+        cross_copies.append(copy)
 
     kv_load = pltpu.make_async_copy(kv_hbm, kv_all.at[seq], kv_own_sem)
     kv_load.start()
@@ -112,16 +149,9 @@
     enc_load.start()
     dec_load = pltpu.make_async_copy(dec_hbm, dec_buf, len_sem.at[1])
     dec_load.start()
-    x_loads = []
-    for c in range(chunks):
-        load = pltpu.make_async_copy(
-            x_hbm.at[:, pl.ds(c * CHUNK, CHUNK)], x_all.at[mp, c], x_sem.at[c]
-        )
-        load.start()
-        x_loads.append(load)
-    order = [mp, pair] + [source for _, source in far]
-    for _, source in far:
-        order.append((source // 2) * 2 + 1 - core)
+    x_load = pltpu.make_async_copy(x_hbm, x_all.at[mp], x_sem)
+    x_load.start()
+    order = [mp, pair] + [source for _, source in far + cross]
     w_loads = []
     for n, piece in enumerate(order):
         start = pl.multiple_of(piece * cols, cols)
@@ -131,43 +161,16 @@
         load.start()
         w_loads.append(load)
 
-    pl.semaphore_wait(barrier, 1 + len(far) + len(ring))
-
-    kv_copies = []
-    for d, (to, _) in enumerate(ring):
-        copy = to_seq(kv_hbm, kv_all.at[seq], kv_s.at[d], kv_r.at[d], to)
-        copy.start()
-        kv_copies.append(copy)
-    far_copies = {}
-    pair_copies = []
-    for c in range(chunks):
-        part = x_hbm.at[:, pl.ds(c * CHUNK, CHUNK)]
-        for d, (to, _) in enumerate(far):
-            copy = to_mp(part, x_all.at[mp, c], far_s.at[d, c], far_r.at[d, c], to)
-            copy.start()
-            far_copies[d, c] = copy
-        copy = to_mp(part, x_all.at[mp, c], pair_s.at[c], pair_r.at[c], pair)
-        copy.start()
-        pair_copies.append(copy)
-
-    def part_of(source, c):
-        return dot(x_all[source, c], w_buf[source, :, c * CHUNK : (c + 1) * CHUNK], NT)
-
-    for load in x_loads:
-        load.wait()
+    def part_of(source, piece):
+        at = slice(*piece)
+        return dot(x_all[source, :, at], w_buf[source, :, at], NT)
+
+    x_load.wait()
     w_loads[0].wait()
-    total = part_of(mp, 0)
-    for c in range(1, chunks):
-        total += part_of(mp, c)
-    g_sum[...] = total
-
-    for copy in pair_copies:
-        copy.wait_recv()
+    g_sum[...] = part_of(mp, (0, cols))
+    pair_copy.wait_recv()
     w_loads[1].wait()
-    total = g_sum[...]
-    for c in range(chunks):
-        total += part_of(pair, c)
-    g_sum[...] = total
+    g_sum[...] += part_of(pair, (0, cols))
 
     kv_load.wait()
     for copy in kv_copies:
@@ -204,24 +207,26 @@
     for load in w_loads[2:]:
         load.wait()
     pass_copies = {}
-    for c in range(chunks + 1):
-        if c < chunks:
-            for d, (_, source) in enumerate(far):
-                far_copies[d, c].wait_recv()
-                slot = x_all.at[source, c]
+    for c, piece in enumerate(pieces):
+        for d, (_, source) in enumerate(far):
+            far_copies[d, c].wait_recv()
+            if c < last:
+                slot = x_all.at[source, :, pl.ds(piece[0], piece[1] - piece[0])]
                 copy = to_mp(slot, slot, pass_s.at[d, c], pass_r.at[d, c], pair)
                 copy.start()
                 pass_copies[d, c] = copy
         total = g_sum[...]
-        if c < chunks:
-            for _, source in far:
-                total += part_of(source, c)
+        for _, source in far:
+            total += part_of(source, piece)
         if c > 0:
-            for d, (_, source) in enumerate(far):
+            for d, (_, source) in enumerate(cross):
                 pass_copies[d, c - 1].wait_recv()
-                total += part_of((source // 2) * 2 + 1 - core, c - 1)
-        if c < chunks:
+                total += part_of(source, pieces[c - 1])
+        if c < last:
             g_sum[...] = total
+    for d, (_, source) in enumerate(cross):
+        cross_copies[d].wait_recv()
+        total += part_of(source, pieces[last])
     g = total.astype(jnp.bfloat16)
 
     value_part = dot(prob_bf16, g, NN)
@@ -257,7 +262,7 @@
     kvg_ref[0] = total[:own].astype(jnp.bfloat16)
     kvg_ref[1] = total[own:].astype(jnp.bfloat16)
 
-    sent = kv_copies + pair_copies + kvg_copies
+    sent = kv_copies + [pair_copy] + cross_copies + kvg_copies
     for copy in sent + list(far_copies.values()) + list(pass_copies.values()):
         copy.wait_send()
 
@@ -277,7 +282,7 @@
     seq_n, mp_n = lax.axis_size("seq"), lax.axis_size("mp")
     rows, width = queries.shape
     cols = out_grad.shape[1]
-    chunks = cols // CHUNK
+    cuts = len(pieces_of(cols))
     own = keys_values.shape[1]
     keys = own * seq_n
     kh = width // DH * keys
@@ -302,7 +307,7 @@
             pltpu.SMEM((SEQS,), jnp.int32),
             pltpu.SMEM((SEQS,), jnp.int32),
             pltpu.VMEM((rows, width), bf16),
-            pltpu.VMEM((mp_n, chunks, rows, CHUNK), bf16),
+            pltpu.VMEM((mp_n, rows, cols), bf16),
             pltpu.VMEM((mp_n, width, cols), bf16),
             pltpu.VMEM((seq_n, 2, own, width), bf16),
             pltpu.VMEM((kh, width), f32),
@@ -312,17 +317,19 @@
             pltpu.VMEM((seq_n, 2 * own, width), f32),
             dma((2,)),
             dma,
-            dma((chunks,)),
+            dma,
             dma((mp_n,)),
             dma,
             dma((seq_n,)),
             dma((seq_n,)),
-            dma((chunks,)),
-            dma((chunks,)),
-            dma((far_n, chunks)),
-            dma((far_n, chunks)),
-            dma((far_n, chunks)),
-            dma((far_n, chunks)),
+            dma,
+            dma,
+            dma((far_n, cuts)),
+            dma((far_n, cuts)),
+            dma((far_n,)),
+            dma((far_n,)),
+            dma((far_n, cuts)),
+            dma((far_n, cuts)),
             dma((seq_n,)),
             dma((seq_n,)),
         ],
@@ -331,6 +338,7 @@
         ),
         name="cross_attention_backward",
     )(*operands)
+    results = [pltpu.with_memory_space_constraint(a, pltpu.VMEM) for a in results]
     return pl.pallas_call(
         store_kernel,
         out_shape=(

time: 20.5 us -> 18.7 us (0.912)
  local copies, waits for them, and re-layouts: 1.23 us -> 0 us
  Pallas kernels: 18.4 us -> 17.9 us
    unnamed x4 -> x0, local copies, waits for them, and re-layouts: 1.23 us -> none
    pallas_call x1, Pallas kernels: 1.58 us -> 0.68 us  [body(): pl.pallas_call(store_kernel, out_shape=(jax.ShapeDtypeStruct((rows, width...]
    pallas_call x1, Pallas kernels: 16.9 us -> 17.2 us  [body(): pl.pallas_call(functools.partial(kernel, seq_n, mp_n), out_shape=(pltpu.V...]
where the time goes in v4:
time: 18.7 us; the launch traced here: 18.5 us
  Pallas kernels  17.9 us (96%)
  between operations  0.64 us (3%)
    pallas_call x1, Pallas kernels, body(): pl.pallas_call(functools.partial(kernel, seq_n, mp_n), out_shape=(pltpu.V...  17.2 us
    pallas_call x1, Pallas kernels, body(): pl.pallas_call(store_kernel, out_shape=(jax.ShapeDtypeStruct((rows, width...  0.68 us

profile of v4, /device:TPU:0, one launch (start us, length us, event | category | flops | bytes accessed | tf_op | source)
XLA Modules:
  0.0 18.5 jit_solution(5518464327708437449)
XLA Ops:
  0.6 17.2 %cross_attention_backward.1 = (bf16[128,512]{1,0:T(8,128)(2,1)S(1)}, bf16[2,2,512]{2,1,0:T(2,128)(2,1)S(1)}) custom-call(s32[2]{0:T(128)} %enc_hbm.1, s32[2]{0:T(128)} %dec_hbm.1, bf16[128,512]{1,0:T(8,128)(2,1)} %q_hbm.1, bf16[2,2,512]{2,1,0:T(2,128)(2,1)} %kv_hbm.1, bf16[128,1024]{1,0:T(8,128)(2,1)} %x_hbm.1, bf16[512,4096]{1,0:T(8,128)(2,1)} %w_hbm.1), custom_call_target="tpu_custom_call" | custom-call | tf_op jit(solution)/shard_map/cross_attention_backward/pallas_call | solution.py:298
  17.9 0.7 %store_results.1 = (bf16[128,512]{1,0:T(8,128)(2,1)}, bf16[2,2,512]{2,1,0:T(2,128)(2,1)}) custom-call(bf16[128,512]{1,0:T(8,128)(2,1)S(1)} %get-tuple-element.4.qg_ref, bf16[2,2,512]{2,1,0:T(2,128)(2,1)S(1)} %get-tuple-element.5.kvg_ref), custom_call_target="tpu_custom_call" | custom-call | tf_op jit(solution)/shard_map/store_results/pallas_call | solution.py:342

commit v5 on v4

--- a/solution.py
+++ b/solution.py
@@ -47,7 +47,7 @@
     kv_all,
     k_rows,
     v_rows,
-    g_sum,
+    vw_buf,
     kvg_send,
     kvg_all,
     len_sem,
@@ -116,6 +116,8 @@
     for to, _ in ring:
         pl.semaphore_signal(barrier, inc=1, device_id=(sec, to, mp), device_id_type=MESH)
 
+    x_load = pltpu.make_async_copy(x_hbm, x_all.at[mp], x_sem)
+    x_load.start()
     pl.semaphore_wait(barrier, 1 + 2 * len(far) + len(ring))
 
     kv_copies = []
@@ -123,21 +125,22 @@
         copy = to_seq(kv_hbm, kv_all.at[seq], kv_s.at[d], kv_r.at[d], to)
         copy.start()
         kv_copies.append(copy)
+    x_load.wait()
     far_copies = {}
     for c, (start, end) in enumerate(pieces):
         at = (slice(None), pl.ds(start, end - start))
         for d, (to, _) in enumerate(far):
-            copy = to_mp(
-                x_hbm.at[at], x_all.at[(mp,) + at], far_s.at[d, c], far_r.at[d, c], to
-            )
+            slot = x_all.at[(mp,) + at]
+            copy = to_mp(slot, slot, far_s.at[d, c], far_r.at[d, c], to)
             copy.start()
             far_copies[d, c] = copy
         if c == 0:
-            pair_copy = to_mp(x_hbm, x_all.at[mp], pair_s, pair_r, pair)
+            pair_copy = to_mp(x_all.at[mp], x_all.at[mp], pair_s, pair_r, pair)
             pair_copy.start()
     cross_copies = []
     for d, (to, _) in enumerate(cross):
-        copy = to_mp(x_hbm.at[at], x_all.at[(mp,) + at], cross_s.at[d], cross_r.at[d], to)
+        slot = x_all.at[(mp,) + at]
+        copy = to_mp(slot, slot, cross_s.at[d], cross_r.at[d], to)
         copy.start()
         cross_copies.append(copy)
 
@@ -149,8 +152,6 @@
     enc_load.start()
     dec_load = pltpu.make_async_copy(dec_hbm, dec_buf, len_sem.at[1])
     dec_load.start()
-    x_load = pltpu.make_async_copy(x_hbm, x_all.at[mp], x_sem)
-    x_load.start()
     order = [mp, pair] + [source for _, source in far + cross]
     w_loads = []
     for n, piece in enumerate(order):
@@ -160,17 +161,6 @@
         )
         load.start()
         w_loads.append(load)
-
-    def part_of(source, piece):
-        at = slice(*piece)
-        return dot(x_all[source, :, at], w_buf[source, :, at], NT)
-
-    x_load.wait()
-    w_loads[0].wait()
-    g_sum[...] = part_of(mp, (0, cols))
-    pair_copy.wait_recv()
-    w_loads[1].wait()
-    g_sum[...] += part_of(pair, (0, cols))
 
     kv_load.wait()
     for copy in kv_copies:
@@ -204,8 +194,26 @@
     prob = jnp.concatenate(probs, axis=0) if heads > 1 else probs[0]
     prob_bf16 = prob.astype(jnp.bfloat16)
 
-    for load in w_loads[2:]:
+    for load, source in zip(w_loads, order):
         load.wait()
+        vw_buf[source] = dot(v_diag, w_buf[source], NN).astype(jnp.bfloat16)
+
+    def parts_of(source, piece):
+        at = slice(*piece)
+        x = x_all[source, :, at]
+        grad_prob = dot(vw_buf[source, :, at], x, NT)
+        weighted = dot(prob_bf16, x, NN).astype(jnp.bfloat16)
+        return grad_prob, dot(weighted, w_buf[source, :, at], NT)
+
+    grad_prob, value_part = parts_of(mp, (0, cols))
+
+    def add(source, piece):
+        more_prob, more_value = parts_of(source, piece)
+        return grad_prob + more_prob, value_part + more_value
+
+    pair_copy.wait_recv()
+    grad_prob, value_part = add(pair, (0, cols))
+
     pass_copies = {}
     for c, piece in enumerate(pieces):
         for d, (_, source) in enumerate(far):
@@ -215,22 +223,16 @@
                 copy = to_mp(slot, slot, pass_s.at[d, c], pass_r.at[d, c], pair)
                 copy.start()
                 pass_copies[d, c] = copy
-        total = g_sum[...]
         for _, source in far:
-            total += part_of(source, piece)
+            grad_prob, value_part = add(source, piece)
         if c > 0:
             for d, (_, source) in enumerate(cross):
                 pass_copies[d, c - 1].wait_recv()
-                total += part_of(source, pieces[c - 1])
-        if c < last:
-            g_sum[...] = total
+                grad_prob, value_part = add(source, pieces[c - 1])
     for d, (_, source) in enumerate(cross):
         cross_copies[d].wait_recv()
-        total += part_of(source, pieces[last])
-    g = total.astype(jnp.bfloat16)
-
-    value_part = dot(prob_bf16, g, NN)
-    grad_prob = dot(v_diag, g, NT)
+        grad_prob, value_part = add(source, pieces[last])
+
     grads = []
     for h in range(heads):
         at = slice(h * keys, (h + 1) * keys)
@@ -312,7 +314,7 @@
             pltpu.VMEM((seq_n, 2, own, width), bf16),
             pltpu.VMEM((kh, width), f32),
             pltpu.VMEM((kh, width), f32),
-            pltpu.VMEM((rows, width), f32),
+            pltpu.VMEM((mp_n, kh, cols), bf16),
             pltpu.VMEM((seq_n, 2 * own, width), f32),
             pltpu.VMEM((seq_n, 2 * own, width), f32),
             dma((2,)),

time: 18.7 us -> 19.4 us (1.037)
  Pallas kernels: 17.9 us -> 18.6 us
    pallas_call x1, Pallas kernels: 17.2 us -> 17.9 us  [body(): pl.pallas_call(functools.partial(kernel, seq_n, mp_n), out_shape=(pltpu.V...]
where the time goes in v5:
time: 19.4 us; the launch traced here: 19.3 us
  Pallas kernels  18.6 us (96%)
  between operations  0.64 us (3%)
    pallas_call x1, Pallas kernels, body(): pl.pallas_call(functools.partial(kernel, seq_n, mp_n), out_shape=(pltpu.V...  17.9 us
    pallas_call x1, Pallas kernels, body(): pl.pallas_call(store_kernel, out_shape=(jax.ShapeDtypeStruct((rows, width...  0.68 us

profile of v5, /device:TPU:0, one launch (start us, length us, event | category | flops | bytes accessed | tf_op | source)
XLA Modules:
  0.0 19.3 jit_solution(1956571853931449455)
XLA Ops:
  0.6 17.9 %cross_attention_backward.1 = (bf16[128,512]{1,0:T(8,128)(2,1)S(1)}, bf16[2,2,512]{2,1,0:T(2,128)(2,1)S(1)}) custom-call(s32[2]{0:T(128)} %enc_hbm.1, s32[2]{0:T(128)} %dec_hbm.1, bf16[128,512]{1,0:T(8,128)(2,1)} %q_hbm.1, bf16[2,2,512]{2,1,0:T(2,128)(2,1)} %kv_hbm.1, bf16[128,1024]{1,0:T(8,128)(2,1)} %x_hbm.1, bf16[512,4096]{1,0:T(8,128)(2,1)} %w_hbm.1), custom_call_target="tpu_custom_call" | custom-call | tf_op jit(solution)/shard_map/cross_attention_backward/pallas_call | solution.py:300
  18.6 0.7 %store_results.1 = (bf16[128,512]{1,0:T(8,128)(2,1)}, bf16[2,2,512]{2,1,0:T(2,128)(2,1)}) custom-call(bf16[128,512]{1,0:T(8,128)(2,1)S(1)} %get-tuple-element.4.qg_ref, bf16[2,2,512]{2,1,0:T(2,128)(2,1)S(1)} %get-tuple-element.5.kvg_ref), custom_call_target="tpu_custom_call" | custom-call | tf_op jit(solution)/shard_map/store_results/pallas_call | solution.py:344

commit v6 on v5

--- a/solution.py
+++ b/solution.py
@@ -120,17 +120,15 @@
     x_load.start()
     pl.semaphore_wait(barrier, 1 + 2 * len(far) + len(ring))
 
-    kv_copies = []
-    for d, (to, _) in enumerate(ring):
-        copy = to_seq(kv_hbm, kv_all.at[seq], kv_s.at[d], kv_r.at[d], to)
-        copy.start()
-        kv_copies.append(copy)
+    half = rows // 2
+    cuts = [(pl.ds(0, rows), pl.ds(a, b - a)) for a, b in pieces[:-1]]
+    tail = pl.ds(pieces[-1][0], pieces[-1][1] - pieces[-1][0])
+    cuts += [(pl.ds(0, half), tail), (pl.ds(half, rows - half), tail)]
     x_load.wait()
     far_copies = {}
-    for c, (start, end) in enumerate(pieces):
-        at = (slice(None), pl.ds(start, end - start))
+    for c, at in enumerate(cuts):
+        slot = x_all.at[(mp,) + at]
         for d, (to, _) in enumerate(far):
-            slot = x_all.at[(mp,) + at]
             copy = to_mp(slot, slot, far_s.at[d, c], far_r.at[d, c], to)
             copy.start()
             far_copies[d, c] = copy
@@ -139,10 +137,16 @@
             pair_copy.start()
     cross_copies = []
     for d, (to, _) in enumerate(cross):
-        slot = x_all.at[(mp,) + at]
+        slot = x_all.at[(mp,) + cuts[-1]]
         copy = to_mp(slot, slot, cross_s.at[d], cross_r.at[d], to)
         copy.start()
         cross_copies.append(copy)
+
+    kv_copies = []
+    for d, (to, _) in enumerate(ring):
+        copy = to_seq(kv_hbm, kv_all.at[seq], kv_s.at[d], kv_r.at[d], to)
+        copy.start()
+        kv_copies.append(copy)
 
     kv_load = pltpu.make_async_copy(kv_hbm, kv_all.at[seq], kv_own_sem)
     kv_load.start()
@@ -215,21 +219,25 @@
     grad_prob, value_part = add(pair, (0, cols))
 
     pass_copies = {}
-    for c, piece in enumerate(pieces):
+    for c, at in enumerate(cuts[:-1]):
         for d, (_, source) in enumerate(far):
             far_copies[d, c].wait_recv()
-            if c < last:
-                slot = x_all.at[source, :, pl.ds(piece[0], piece[1] - piece[0])]
-                copy = to_mp(slot, slot, pass_s.at[d, c], pass_r.at[d, c], pair)
-                copy.start()
-                pass_copies[d, c] = copy
-        for _, source in far:
-            grad_prob, value_part = add(source, piece)
+            slot = x_all.at[(source,) + at]
+            copy = to_mp(slot, slot, pass_s.at[d, c], pass_r.at[d, c], pair)
+            copy.start()
+            pass_copies[d, c] = copy
+        if c < last:
+            for _, source in far:
+                grad_prob, value_part = add(source, pieces[c])
         if c > 0:
             for d, (_, source) in enumerate(cross):
                 pass_copies[d, c - 1].wait_recv()
                 grad_prob, value_part = add(source, pieces[c - 1])
+    for d, (_, source) in enumerate(far):
+        far_copies[d, last + 1].wait_recv()
+        grad_prob, value_part = add(source, pieces[last])
     for d, (_, source) in enumerate(cross):
+        pass_copies[d, last].wait_recv()
         cross_copies[d].wait_recv()
         grad_prob, value_part = add(source, pieces[last])
 
@@ -247,8 +255,9 @@
 
     key_part, value_part = own_head(key_part), own_head(value_part)
     for t in range(seq_n):
-        kvg_send[t, pl.ds(0, own), :] = key_part[t * own : (t + 1) * own]
-        kvg_send[t, pl.ds(own, own), :] = value_part[t * own : (t + 1) * own]
+        at = slice(t * own, (t + 1) * own)
+        kvg_send[t, 0] = key_part[at].astype(jnp.bfloat16)
+        kvg_send[t, 1] = value_part[at].astype(jnp.bfloat16)
     kvg_copies = []
     for d, (to, _) in enumerate(ring):
         copy = to_seq(kvg_send.at[to], kvg_all.at[seq], kvg_s.at[d], kvg_r.at[d], to)
@@ -257,15 +266,17 @@
 
     qg_ref[...] = (dot(grad_score, k_diag, TN) * scale).astype(jnp.bfloat16)
 
-    total = kvg_send[seq]
+    sent = kv_copies + [pair_copy] + cross_copies
+    for copy in sent + list(far_copies.values()) + list(pass_copies.values()):
+        copy.wait_send()
+
+    sums = [kvg_send[seq, n].astype(jnp.float32) for n in range(2)]
     for d, (_, source) in enumerate(ring):
         kvg_copies[d].wait_recv()
-        total += kvg_all[source]
-    kvg_ref[0] = total[:own].astype(jnp.bfloat16)
-    kvg_ref[1] = total[own:].astype(jnp.bfloat16)
-
-    sent = kv_copies + [pair_copy] + cross_copies + kvg_copies
-    for copy in sent + list(far_copies.values()) + list(pass_copies.values()):
+        sums = [sums[n] + kvg_all[source, n].astype(jnp.float32) for n in range(2)]
+    for n in range(2):
+        kvg_ref[n] = sums[n].astype(jnp.bfloat16)
+    for copy in kvg_copies:
         copy.wait_send()
 
 
@@ -284,7 +295,7 @@
     seq_n, mp_n = lax.axis_size("seq"), lax.axis_size("mp")
     rows, width = queries.shape
     cols = out_grad.shape[1]
-    cuts = len(pieces_of(cols))
+    cuts = len(pieces_of(cols)) + 1
     own = keys_values.shape[1]
     keys = own * seq_n
     kh = width // DH * keys
@@ -315,8 +326,8 @@
             pltpu.VMEM((kh, width), f32),
             pltpu.VMEM((kh, width), f32),
             pltpu.VMEM((mp_n, kh, cols), bf16),
-            pltpu.VMEM((seq_n, 2 * own, width), f32),
-            pltpu.VMEM((seq_n, 2 * own, width), f32),
+            pltpu.VMEM((seq_n, 2, own, width), bf16),
+            pltpu.VMEM((seq_n, 2, own, width), bf16),
             dma((2,)),
             dma,
             dma,

time: 19.4 us -> 19.5 us (level)
  no operation moved by 1% of the time
where the time goes in v6:
time: 19.5 us; the launch traced here: 19.3 us
  Pallas kernels  18.7 us (96%)
  between operations  0.64 us (3%)
    pallas_call x1, Pallas kernels, body(): pl.pallas_call(functools.partial(kernel, seq_n, mp_n), out_shape=(pltpu.V...  18 us
    pallas_call x1, Pallas kernels, body(): pl.pallas_call(store_kernel, out_shape=(jax.ShapeDtypeStruct((rows, width...  0.68 us

profile of v6, /device:TPU:0, one launch (start us, length us, event | category | flops | bytes accessed | tf_op | source)
XLA Modules:
  0.0 19.3 jit_solution(12878591125578595195)
XLA Ops:
  0.6 18.0 %cross_attention_backward.1 = (bf16[128,512]{1,0:T(8,128)(2,1)S(1)}, bf16[2,2,512]{2,1,0:T(2,128)(2,1)S(1)}) custom-call(s32[2]{0:T(128)} %enc_hbm.1, s32[2]{0:T(128)} %dec_hbm.1, bf16[128,512]{1,0:T(8,128)(2,1)} %q_hbm.1, bf16[2,2,512]{2,1,0:T(2,128)(2,1)} %kv_hbm.1, bf16[128,1024]{1,0:T(8,128)(2,1)} %x_hbm.1, bf16[512,4096]{1,0:T(8,128)(2,1)} %w_hbm.1), custom_call_target="tpu_custom_call" | custom-call | tf_op jit(solution)/shard_map/cross_attention_backward/pallas_call | solution.py:311
  18.7 0.7 %store_results.1 = (bf16[128,512]{1,0:T(8,128)(2,1)}, bf16[2,2,512]{2,1,0:T(2,128)(2,1)}) custom-call(bf16[128,512]{1,0:T(8,128)(2,1)S(1)} %get-tuple-element.4.qg_ref, bf16[2,2,512]{2,1,0:T(2,128)(2,1)S(1)} %get-tuple-element.5.kvg_ref), custom_call_target="tpu_custom_call" | custom-call | tf_op jit(solution)/shard_map/store_results/pallas_call | solution.py:355

commit v7 on v5

--- a/solution.py
+++ b/solution.py
@@ -118,6 +118,24 @@
 
     x_load = pltpu.make_async_copy(x_hbm, x_all.at[mp], x_sem)
     x_load.start()
+    kv_load = pltpu.make_async_copy(kv_hbm, kv_all.at[seq], kv_own_sem)
+    kv_load.start()
+    q_load = pltpu.make_async_copy(q_hbm, q_buf, q_sem)
+    q_load.start()
+    enc_load = pltpu.make_async_copy(enc_hbm, enc_buf, len_sem.at[0])
+    enc_load.start()
+    dec_load = pltpu.make_async_copy(dec_hbm, dec_buf, len_sem.at[1])
+    dec_load.start()
+    order = [mp, pair] + [source for _, source in far + cross]
+    w_loads = []
+    for n, piece in enumerate(order):
+        start = pl.multiple_of(piece * cols, cols)
+        load = pltpu.make_async_copy(
+            w_hbm.at[:, pl.ds(start, cols)], w_buf.at[piece], w_sem.at[n]
+        )
+        load.start(priority=1)
+        w_loads.append(load)
+
     pl.semaphore_wait(barrier, 1 + 2 * len(far) + len(ring))
 
     kv_copies = []
@@ -144,24 +162,6 @@
         copy.start()
         cross_copies.append(copy)
 
-    kv_load = pltpu.make_async_copy(kv_hbm, kv_all.at[seq], kv_own_sem)
-    kv_load.start()
-    q_load = pltpu.make_async_copy(q_hbm, q_buf, q_sem)
-    q_load.start()
-    enc_load = pltpu.make_async_copy(enc_hbm, enc_buf, len_sem.at[0])
-    enc_load.start()
-    dec_load = pltpu.make_async_copy(dec_hbm, dec_buf, len_sem.at[1])
-    dec_load.start()
-    order = [mp, pair] + [source for _, source in far + cross]
-    w_loads = []
-    for n, piece in enumerate(order):
-        start = pl.multiple_of(piece * cols, cols)
-        load = pltpu.make_async_copy(
-            w_hbm.at[:, pl.ds(start, cols)], w_buf.at[piece], w_sem.at[n]
-        )
-        load.start()
-        w_loads.append(load)
-
     kv_load.wait()
     for copy in kv_copies:
         copy.wait_recv()
@@ -257,6 +257,10 @@
 
     qg_ref[...] = (dot(grad_score, k_diag, TN) * scale).astype(jnp.bfloat16)
 
+    sent = kv_copies + [pair_copy] + cross_copies
+    for copy in sent + list(far_copies.values()) + list(pass_copies.values()):
+        copy.wait_send()
+
     total = kvg_send[seq]
     for d, (_, source) in enumerate(ring):
         kvg_copies[d].wait_recv()
@@ -264,8 +268,7 @@
     kvg_ref[0] = total[:own].astype(jnp.bfloat16)
     kvg_ref[1] = total[own:].astype(jnp.bfloat16)
 
-    sent = kv_copies + [pair_copy] + cross_copies + kvg_copies
-    for copy in sent + list(far_copies.values()) + list(pass_copies.values()):
+    for copy in kvg_copies:
         copy.wait_send()
 
 

time: 19.4 us -> 19.4 us (level)
  no operation moved by 1% of the time
where the time goes in v7:
time: 19.4 us; the launch traced here: 19.2 us
  Pallas kernels  18.6 us (96%)
  between operations  0.64 us (3%)
    pallas_call x1, Pallas kernels, body(): pl.pallas_call(functools.partial(kernel, seq_n, mp_n), out_shape=(pltpu.V...  17.9 us
    pallas_call x1, Pallas kernels, body(): pl.pallas_call(store_kernel, out_shape=(jax.ShapeDtypeStruct((rows, width...  0.68 us

profile of v7, /device:TPU:0, one launch (start us, length us, event | category | flops | bytes accessed | tf_op | source)
XLA Modules:
  0.0 19.2 jit_solution(6781687960451441828)
XLA Ops:
  0.6 17.9 %cross_attention_backward.1 = (bf16[128,512]{1,0:T(8,128)(2,1)S(1)}, bf16[2,2,512]{2,1,0:T(2,128)(2,1)S(1)}) custom-call(s32[2]{0:T(128)} %enc_hbm.1, s32[2]{0:T(128)} %dec_hbm.1, bf16[128,512]{1,0:T(8,128)(2,1)} %q_hbm.1, bf16[2,2,512]{2,1,0:T(2,128)(2,1)} %kv_hbm.1, bf16[128,1024]{1,0:T(8,128)(2,1)} %x_hbm.1, bf16[512,4096]{1,0:T(8,128)(2,1)} %w_hbm.1), custom_call_target="tpu_custom_call" | custom-call | tf_op jit(solution)/shard_map/cross_attention_backward/pallas_call | solution.py:303
  18.6 0.7 %store_results.1 = (bf16[128,512]{1,0:T(8,128)(2,1)}, bf16[2,2,512]{2,1,0:T(2,128)(2,1)}) custom-call(bf16[128,512]{1,0:T(8,128)(2,1)S(1)} %get-tuple-element.4.qg_ref, bf16[2,2,512]{2,1,0:T(2,128)(2,1)S(1)} %get-tuple-element.5.kvg_ref), custom_call_target="tpu_custom_call" | custom-call | tf_op jit(solution)/shard_map/store_results/pallas_call | solution.py:347

commit v8 on v5

--- a/solution.py
+++ b/solution.py
@@ -116,8 +116,6 @@
     for to, _ in ring:
         pl.semaphore_signal(barrier, inc=1, device_id=(sec, to, mp), device_id_type=MESH)
 
-    x_load = pltpu.make_async_copy(x_hbm, x_all.at[mp], x_sem)
-    x_load.start()
     pl.semaphore_wait(barrier, 1 + 2 * len(far) + len(ring))
 
     kv_copies = []
@@ -125,25 +123,26 @@
         copy = to_seq(kv_hbm, kv_all.at[seq], kv_s.at[d], kv_r.at[d], to)
         copy.start()
         kv_copies.append(copy)
-    x_load.wait()
     far_copies = {}
     for c, (start, end) in enumerate(pieces):
         at = (slice(None), pl.ds(start, end - start))
         for d, (to, _) in enumerate(far):
-            slot = x_all.at[(mp,) + at]
-            copy = to_mp(slot, slot, far_s.at[d, c], far_r.at[d, c], to)
+            copy = to_mp(
+                x_hbm.at[at], x_all.at[(mp,) + at], far_s.at[d, c], far_r.at[d, c], to
+            )
             copy.start()
             far_copies[d, c] = copy
         if c == 0:
-            pair_copy = to_mp(x_all.at[mp], x_all.at[mp], pair_s, pair_r, pair)
+            pair_copy = to_mp(x_hbm, x_all.at[mp], pair_s, pair_r, pair)
             pair_copy.start()
     cross_copies = []
     for d, (to, _) in enumerate(cross):
-        slot = x_all.at[(mp,) + at]
-        copy = to_mp(slot, slot, cross_s.at[d], cross_r.at[d], to)
+        copy = to_mp(x_hbm.at[at], x_all.at[(mp,) + at], cross_s.at[d], cross_r.at[d], to)
         copy.start()
         cross_copies.append(copy)
 
+    x_load = pltpu.make_async_copy(x_hbm, x_all.at[mp], x_sem)
+    x_load.start()
     kv_load = pltpu.make_async_copy(kv_hbm, kv_all.at[seq], kv_own_sem)
     kv_load.start()
     q_load = pltpu.make_async_copy(q_hbm, q_buf, q_sem)
@@ -159,7 +158,7 @@
         load = pltpu.make_async_copy(
             w_hbm.at[:, pl.ds(start, cols)], w_buf.at[piece], w_sem.at[n]
         )
-        load.start()
+        load.start(priority=1)
         w_loads.append(load)
 
     kv_load.wait()
@@ -205,6 +204,7 @@
         weighted = dot(prob_bf16, x, NN).astype(jnp.bfloat16)
         return grad_prob, dot(weighted, w_buf[source, :, at], NT)
 
+    x_load.wait()
     grad_prob, value_part = parts_of(mp, (0, cols))
 
     def add(source, piece):
@@ -257,6 +257,10 @@
 
     qg_ref[...] = (dot(grad_score, k_diag, TN) * scale).astype(jnp.bfloat16)
 
+    sent = kv_copies + [pair_copy] + cross_copies
+    for copy in sent + list(far_copies.values()) + list(pass_copies.values()):
+        copy.wait_send()
+
     total = kvg_send[seq]
     for d, (_, source) in enumerate(ring):
         kvg_copies[d].wait_recv()
@@ -264,8 +268,7 @@
     kvg_ref[0] = total[:own].astype(jnp.bfloat16)
     kvg_ref[1] = total[own:].astype(jnp.bfloat16)
 
-    sent = kv_copies + [pair_copy] + cross_copies + kvg_copies
-    for copy in sent + list(far_copies.values()) + list(pass_copies.values()):
+    for copy in kvg_copies:
         copy.wait_send()
 
 

time: 19.4 us -> 19.5 us (level)
  no operation moved by 1% of the time
where the time goes in v8:
time: 19.5 us; the launch traced here: 19.4 us
  Pallas kernels  18.7 us (96%)
  between operations  0.64 us (3%)
    pallas_call x1, Pallas kernels, body(): pl.pallas_call(functools.partial(kernel, seq_n, mp_n), out_shape=(pltpu.V...  18 us
    pallas_call x1, Pallas kernels, body(): pl.pallas_call(store_kernel, out_shape=(jax.ShapeDtypeStruct((rows, width...  0.68 us

profile of v8, /device:TPU:0, one launch (start us, length us, event | category | flops | bytes accessed | tf_op | source)
XLA Modules:
  0.0 19.4 jit_solution(3887831751877846925)
XLA Ops:
  0.6 18.0 %cross_attention_backward.1 = (bf16[128,512]{1,0:T(8,128)(2,1)S(1)}, bf16[2,2,512]{2,1,0:T(2,128)(2,1)S(1)}) custom-call(s32[2]{0:T(128)} %enc_hbm.1, s32[2]{0:T(128)} %dec_hbm.1, bf16[128,512]{1,0:T(8,128)(2,1)} %q_hbm.1, bf16[2,2,512]{2,1,0:T(2,128)(2,1)} %kv_hbm.1, bf16[128,1024]{1,0:T(8,128)(2,1)} %x_hbm.1, bf16[512,4096]{1,0:T(8,128)(2,1)} %w_hbm.1), custom_call_target="tpu_custom_call" | custom-call | tf_op jit(solution)/shard_map/cross_attention_backward/pallas_call | solution.py:303
  18.7 0.7 %store_results.1 = (bf16[128,512]{1,0:T(8,128)(2,1)}, bf16[2,2,512]{2,1,0:T(2,128)(2,1)}) custom-call(bf16[128,512]{1,0:T(8,128)(2,1)S(1)} %get-tuple-element.4.qg_ref, bf16[2,2,512]{2,1,0:T(2,128)(2,1)S(1)} %get-tuple-element.5.kvg_ref), custom_call_target="tpu_custom_call" | custom-call | tf_op jit(solution)/shard_map/store_results/pallas_call | solution.py:347

commit v9 on v4

--- a/solution.py
+++ b/solution.py
@@ -20,12 +20,8 @@
     return lax.dot_general(a, b, dims, preferred_element_type=jnp.float32)
 
 
-def pieces_of(cols):
-    edges = list(range(0, cols, max(cols // 4, LANES))) + [cols]
-    middle = (edges[-2] + cols) // 2
-    if middle % LANES == 0 and middle > edges[-2]:
-        edges.insert(-1, middle)
-    return list(zip(edges[:-1], edges[1:]))
+def piece_of(cols):
+    return max(cols // 4, LANES)
 
 
 def kernel(
@@ -61,8 +57,6 @@
     pair_r,
     far_s,
     far_r,
-    cross_s,
-    cross_r,
     pass_s,
     pass_r,
     kvg_s,
@@ -73,8 +67,8 @@
     mp = lax.axis_index("mp")
     rows, width = q_buf.shape
     cols = x_all.shape[2]
-    pieces = pieces_of(cols)
-    last = len(pieces) - 1
+    piece = piece_of(cols)
+    pieces = cols // piece
     own = kv_hbm.shape[1]
     heads = width // DH
     keys = own * seq_n
@@ -111,12 +105,12 @@
         )
 
     barrier = pltpu.get_barrier_semaphore()
-    for to in [pair] + [to for to, _ in far + cross]:
+    for to in [pair] + [to for to, _ in far]:
         pl.semaphore_signal(barrier, inc=1, device_id=(sec, seq, to), device_id_type=MESH)
     for to, _ in ring:
         pl.semaphore_signal(barrier, inc=1, device_id=(sec, to, mp), device_id_type=MESH)
 
-    pl.semaphore_wait(barrier, 1 + 2 * len(far) + len(ring))
+    pl.semaphore_wait(barrier, 1 + len(far) + len(ring))
 
     kv_copies = []
     for d, (to, _) in enumerate(ring):
@@ -124,8 +118,8 @@
         copy.start()
         kv_copies.append(copy)
     far_copies = {}
-    for c, (start, end) in enumerate(pieces):
-        at = (slice(None), pl.ds(start, end - start))
+    for c in range(pieces):
+        at = (slice(None), pl.ds(c * piece, piece))
         for d, (to, _) in enumerate(far):
             copy = to_mp(
                 x_hbm.at[at], x_all.at[(mp,) + at], far_s.at[d, c], far_r.at[d, c], to
@@ -135,12 +129,6 @@
         if c == 0:
             pair_copy = to_mp(x_hbm, x_all.at[mp], pair_s, pair_r, pair)
             pair_copy.start()
-    cross_copies = []
-    for d, (to, _) in enumerate(cross):
-        copy = to_mp(x_hbm.at[at], x_all.at[(mp,) + at], cross_s.at[d], cross_r.at[d], to)
-        copy.start()
-        cross_copies.append(copy)
-
     kv_load = pltpu.make_async_copy(kv_hbm, kv_all.at[seq], kv_own_sem)
     kv_load.start()
     q_load = pltpu.make_async_copy(q_hbm, q_buf, q_sem)
@@ -153,24 +141,32 @@
     x_load.start()
     order = [mp, pair] + [source for _, source in far + cross]
     w_loads = []
-    for n, piece in enumerate(order):
-        start = pl.multiple_of(piece * cols, cols)
+    for n, source in enumerate(order):
+        start = pl.multiple_of(source * cols, cols)
         load = pltpu.make_async_copy(
-            w_hbm.at[:, pl.ds(start, cols)], w_buf.at[piece], w_sem.at[n]
+            w_hbm.at[:, pl.ds(start, cols)], w_buf.at[source], w_sem.at[n]
         )
         load.start()
         w_loads.append(load)
 
-    def part_of(source, piece):
-        at = slice(*piece)
-        return dot(x_all[source, :, at], w_buf[source, :, at], NT)
-
+    def columns(c):
+        return pl.ds(pl.multiple_of(c * piece, piece), piece)
+
+    def add(source, c):
+        at = columns(c)
+        g_sum[...] += dot(x_all[source, :, at], w_buf[source, :, at], NT)
+
+    g_sum[...] = jnp.zeros_like(g_sum)
     x_load.wait()
-    w_loads[0].wait()
-    g_sum[...] = part_of(mp, (0, cols))
     pair_copy.wait_recv()
-    w_loads[1].wait()
-    g_sum[...] += part_of(pair, (0, cols))
+    for load in w_loads[:2]:
+        load.wait()
+
+    def near_step(n, carry):
+        add(jnp.where(n < pieces, mp, pair), lax.rem(n, pieces))
+        return carry
+
+    lax.fori_loop(0, 2 * pieces, near_step, 0)
 
     kv_load.wait()
     for copy in kv_copies:
@@ -206,28 +202,28 @@
 
     for load in w_loads[2:]:
         load.wait()
-    pass_copies = {}
-    for c, piece in enumerate(pieces):
-        for d, (_, source) in enumerate(far):
-            far_copies[d, c].wait_recv()
-            if c < last:
-                slot = x_all.at[source, :, pl.ds(piece[0], piece[1] - piece[0])]
-                copy = to_mp(slot, slot, pass_s.at[d, c], pass_r.at[d, c], pair)
-                copy.start()
-                pass_copies[d, c] = copy
-        total = g_sum[...]
+
+    def handing_on(d, c):
+        slot = x_all.at[far[d][1], :, columns(c)]
+        return to_mp(slot, slot, pass_s.at[d, c], pass_r.at[d, c], pair)
+
+    def arriving(d, c):
+        slot = x_all.at[far[d][1], :, columns(c)]
+        return to_mp(slot, slot, far_s.at[d, c], far_r.at[d, c], far[d][0])
+
+    def far_step(c, carry):
+        for d in range(len(far)):
+            arriving(d, c).wait_recv()
+            handing_on(d, c).start()
         for _, source in far:
-            total += part_of(source, piece)
-        if c > 0:
-            for d, (_, source) in enumerate(cross):
-                pass_copies[d, c - 1].wait_recv()
-                total += part_of(source, pieces[c - 1])
-        if c < last:
-            g_sum[...] = total
-    for d, (_, source) in enumerate(cross):
-        cross_copies[d].wait_recv()
-        total += part_of(source, pieces[last])
-    g = total.astype(jnp.bfloat16)
+            add(source, c)
+        for d, (_, source) in enumerate(cross):
+            handing_on(d, c).wait_recv()
+            add(source, c)
+        return carry
+
+    lax.fori_loop(0, pieces, far_step, 0)
+    g = g_sum[...].astype(jnp.bfloat16)
 
     value_part = dot(prob_bf16, g, NN)
     grad_prob = dot(v_diag, g, NT)
@@ -255,6 +251,12 @@
 
     qg_ref[...] = (dot(grad_score, k_diag, TN) * scale).astype(jnp.bfloat16)
 
+    for copy in kv_copies + [pair_copy] + list(far_copies.values()):
+        copy.wait_send()
+    for d in range(len(far)):
+        for c in range(pieces):
+            handing_on(d, c).wait_send()
+
     total = kvg_send[seq]
     for d, (_, source) in enumerate(ring):
         kvg_copies[d].wait_recv()
@@ -262,8 +264,7 @@
     kvg_ref[0] = total[:own].astype(jnp.bfloat16)
     kvg_ref[1] = total[own:].astype(jnp.bfloat16)
 
-    sent = kv_copies + [pair_copy] + cross_copies + kvg_copies
-    for copy in sent + list(far_copies.values()) + list(pass_copies.values()):
+    for copy in kvg_copies:
         copy.wait_send()
 
 
@@ -282,7 +283,7 @@
     seq_n, mp_n = lax.axis_size("seq"), lax.axis_size("mp")
     rows, width = queries.shape
     cols = out_grad.shape[1]
-    cuts = len(pieces_of(cols))
+    cuts = cols // piece_of(cols)
     own = keys_values.shape[1]
     keys = own * seq_n
     kh = width // DH * keys
@@ -326,8 +327,6 @@
             dma,
             dma((far_n, cuts)),
             dma((far_n, cuts)),
-            dma((far_n,)),
-            dma((far_n,)),
             dma((far_n, cuts)),
             dma((far_n, cuts)),
             dma((seq_n,)),

time: 18.7 us -> 19.8 us (1.059)
  Pallas kernels: 17.9 us -> 19 us
    pallas_call x1, Pallas kernels: 17.2 us -> 18.4 us  [body(): pl.pallas_call(functools.partial(kernel, seq_n, mp_n), out_shape=(pltpu.V...]
where the time goes in v9:
time: 19.8 us; the launch traced here: 19.7 us
  Pallas kernels  19 us (96%)
  between operations  0.64 us (3%)
    pallas_call x1, Pallas kernels, body(): pl.pallas_call(functools.partial(kernel, seq_n, mp_n), out_shape=(pltpu.V...  18.4 us
    pallas_call x1, Pallas kernels, body(): pl.pallas_call(store_kernel, out_shape=(jax.ShapeDtypeStruct((rows, width...  0.68 us

profile of v9, /device:TPU:0, one launch (start us, length us, event | category | flops | bytes accessed | tf_op | source)
XLA Modules:
  0.0 19.7 jit_solution(8306689775634878808)
XLA Ops:
  0.6 18.4 %cross_attention_backward.1 = (bf16[128,512]{1,0:T(8,128)(2,1)S(1)}, bf16[2,2,512]{2,1,0:T(2,128)(2,1)S(1)}) custom-call(s32[2]{0:T(128)} %enc_hbm.1, s32[2]{0:T(128)} %dec_hbm.1, bf16[128,512]{1,0:T(8,128)(2,1)} %q_hbm.1, bf16[2,2,512]{2,1,0:T(2,128)(2,1)} %kv_hbm.1, bf16[128,1024]{1,0:T(8,128)(2,1)} %x_hbm.1, bf16[512,4096]{1,0:T(8,128)(2,1)} %w_hbm.1), custom_call_target="tpu_custom_call" | custom-call | tf_op jit(solution)/shard_map/cross_attention_backward/pallas_call | solution.py:299
  19.0 0.7 %store_results.1 = (bf16[128,512]{1,0:T(8,128)(2,1)}, bf16[2,2,512]{2,1,0:T(2,128)(2,1)}) custom-call(bf16[128,512]{1,0:T(8,128)(2,1)S(1)} %get-tuple-element.4.qg_ref, bf16[2,2,512]{2,1,0:T(2,128)(2,1)S(1)} %get-tuple-element.5.kvg_ref), custom_call_target="tpu_custom_call" | custom-call | tf_op jit(solution)/shard_map/store_results/pallas_call | solution.py:341

commit v10 on v4

--- a/solution.py
+++ b/solution.py
@@ -158,7 +158,7 @@
         load = pltpu.make_async_copy(
             w_hbm.at[:, pl.ds(start, cols)], w_buf.at[piece], w_sem.at[n]
         )
-        load.start()
+        load.start(priority=1)
         w_loads.append(load)
 
     def part_of(source, piece):
@@ -255,6 +255,10 @@
 
     qg_ref[...] = (dot(grad_score, k_diag, TN) * scale).astype(jnp.bfloat16)
 
+    sent = kv_copies + [pair_copy] + cross_copies
+    for copy in sent + list(far_copies.values()) + list(pass_copies.values()):
+        copy.wait_send()
+
     total = kvg_send[seq]
     for d, (_, source) in enumerate(ring):
         kvg_copies[d].wait_recv()
@@ -262,8 +266,7 @@
     kvg_ref[0] = total[:own].astype(jnp.bfloat16)
     kvg_ref[1] = total[own:].astype(jnp.bfloat16)
 
-    sent = kv_copies + [pair_copy] + cross_copies + kvg_copies
-    for copy in sent + list(far_copies.values()) + list(pass_copies.values()):
+    for copy in kvg_copies:
         copy.wait_send()
 
 

time: 18.7 us -> 18.7 us (level)
  no operation moved by 1% of the time
where the time goes in v10:
time: 18.7 us; the launch traced here: 18.5 us
  Pallas kernels  17.9 us (96%)
  between operations  0.64 us (3%)
    pallas_call x1, Pallas kernels, body(): pl.pallas_call(functools.partial(kernel, seq_n, mp_n), out_shape=(pltpu.V...  17.2 us
    pallas_call x1, Pallas kernels, body(): pl.pallas_call(store_kernel, out_shape=(jax.ShapeDtypeStruct((rows, width...  0.68 us

profile of v10, /device:TPU:0, one launch (start us, length us, event | category | flops | bytes accessed | tf_op | source)
XLA Modules:
  0.0 18.5 jit_solution(6103608132115314886)
XLA Ops:
  0.6 17.2 %cross_attention_backward.1 = (bf16[128,512]{1,0:T(8,128)(2,1)S(1)}, bf16[2,2,512]{2,1,0:T(2,128)(2,1)S(1)}) custom-call(s32[2]{0:T(128)} %enc_hbm.1, s32[2]{0:T(128)} %dec_hbm.1, bf16[128,512]{1,0:T(8,128)(2,1)} %q_hbm.1, bf16[2,2,512]{2,1,0:T(2,128)(2,1)} %kv_hbm.1, bf16[128,1024]{1,0:T(8,128)(2,1)} %x_hbm.1, bf16[512,4096]{1,0:T(8,128)(2,1)} %w_hbm.1), custom_call_target="tpu_custom_call" | custom-call | tf_op jit(solution)/shard_map/cross_attention_backward/pallas_call | solution.py:301
  17.8 0.7 %store_results.1 = (bf16[128,512]{1,0:T(8,128)(2,1)}, bf16[2,2,512]{2,1,0:T(2,128)(2,1)}) custom-call(bf16[128,512]{1,0:T(8,128)(2,1)S(1)} %get-tuple-element.4.qg_ref, bf16[2,2,512]{2,1,0:T(2,128)(2,1)S(1)} %get-tuple-element.5.kvg_ref), custom_call_target="tpu_custom_call" | custom-call | tf_op jit(solution)/shard_map/store_results/pallas_call | solution.py:345
